TPU v7x, 128 devices: a whole 4x4x4 slice. The times are simulated.
128 devices in a mesh: gx: 32 (over z, x, core), gz: 4 (over y).
Axes of the slice: x: 4, y: 4, z: 4, core: 2. Of those that a mesh axis runs over, the one named last changes fastest.
Arguments:
- heads: bfloat16 [16, 4, 2048, 2048], P(None, 'gz', 'gx'), may hold values from -6 to 6
- leak: float32 [4, 2048, 2048], P('gz', 'gx'), may hold values from 0.05 to 0.3
- x_inverse: bfloat16 [4, 2048, 2048], P('gz')
- y_inverse: bfloat16 [4, 2048, 2048], P('gz')
- misfit: float32 [32768, 16], P(('gx', 'gz')), may hold values from -6 to 6
- row_owner: int32 [32768, 1], P(('gx', 'gz')), may hold values from 0 to 127; in each aligned block of 256 rows (0 to 255, 256 to 511, ...) at most 4 rows name the same one
- row_count: int32 [128], P(('gx', 'gz')), may hold values from 1 to 256, 16384 in all
- row_x: int32 [32768], P(('gx', 'gz')), may hold values from 0 to 63
- row_seg: int32 [32768], P(('gx', 'gz')), may hold values from 0 to 15
Outputs:
- adjoint: bfloat16 [16, 4, 2048, 2048], P(None, 'gz', 'gx')
- gradient: float32 [128, 16, 128], P(('gx', 'gz'))
Inputs may be any that keep to these rules, and one draw needn't show every extreme that they name: `row_owner`: within the rows of one device (aligned blocks of 256 rows) no owner is named by more than 4 rows, a bound that some block reaches. Only the first row_count[d] rows of device d are live.
All inputs are finite; a program needn't handle non-finite values.
Results may differ from a plain program's by a relative error of at most 0.0057.
Values may be sent and summed in bfloat16 or wider, within the bound.
No kernel may reach another device: no remote copies, remote signals or barrier semaphores. Data moves between devices by JAX's collectives and lax.ppermute only.
A program may use at most 128 MiB of HBM per device.

v0:
```python
import jax
import jax.numpy as jnp
from jax import lax
from jax.sharding import PartitionSpec as P

SEG = 128


def padded_2(cells, sides, width):
    for axis, dim in sides:
        count = lax.axis_size(axis)
        ends = count - 1
        head = lax.slice_in_dim(cells, 0, width, axis=dim)
        tail = lax.slice_in_dim(cells, cells.shape[dim] - width, cells.shape[dim], axis=dim)
        cells = jnp.concatenate(
            [
                lax.ppermute(tail, axis, [(i, (i + 1) % count) for i in range(ends)]),
                cells,
                lax.ppermute(head, axis, [((i + 1) % count, i) for i in range(ends)]),
            ],
            axis=dim,
        )
    return cells


def body(heads, leak, x_inverse, y_inverse, misfit, row_owner, row_count, row_x, row_seg):
    padded = padded_2(heads, (("gz", 1),), 1)
    centre = heads.astype(jnp.float32)
    vertical = (
        centre
        + leak[None]
        * (padded[:, 2:].astype(jnp.float32) + padded[:, :-2].astype(jnp.float32) - 2.0 * centre)
    ).astype(jnp.bfloat16)
    x_swept = jnp.einsum(
        "tzyj,zij->tzyi", vertical, x_inverse, preferred_element_type=jnp.float32
    ).astype(jnp.bfloat16)
    adjoint = jnp.einsum(
        "tzjx,zij->tzxi",
        lax.all_to_all(x_swept, "gx", split_axis=3, concat_axis=2, tiled=True),
        y_inverse,
        preferred_element_type=jnp.float32,
    ).astype(jnp.bfloat16)
    test_count = adjoint.shape[0]
    x_local = adjoint.shape[2]
    segments = adjoint.shape[3] // SEG
    row_total = row_x.shape[0]
    blocks = adjoint.reshape(test_count, x_local * segments, SEG)
    row_index = row_x * segments + row_seg
    picked = jnp.take(blocks, row_index, axis=1).astype(jnp.float32)
    live_rows = (jnp.arange(row_total, dtype=jnp.int32) < row_count[0]).astype(jnp.float32)
    weighted = picked * (jnp.transpose(misfit) * live_rows[None, :])[:, :, None]
    gx_count = lax.axis_size("gx")
    gz_count = lax.axis_size("gz")
    device_total = gx_count * gz_count
    owners = row_owner[:, 0]
    onehot = (owners[:, None] == jnp.arange(device_total, dtype=jnp.int32)[None, :]).astype(
        jnp.int32
    )
    buffer = jnp.einsum(
        "rk,trs->kts", onehot.astype(jnp.float32), weighted, precision=lax.Precision.HIGHEST
    )
    buffer = buffer.reshape(device_total, 1, test_count, SEG)
    arrived = lax.all_to_all(buffer, ("gx", "gz"), split_axis=0, concat_axis=0, tiled=True)
    summed = jnp.sum(arrived, axis=(0, 1))
    return (adjoint, summed[None])


def solution(mesh):
    placed = (
        P(None, "gz", "gx", None),
        P("gz", "gx", None),
        P("gz", None, None),
        P("gz", None, None),
        P(("gx", "gz"), None),
        P(("gx", "gz"), None),
        P(("gx", "gz")),
        P(("gx", "gz")),
        P(("gx", "gz")),
    )
    return jax.shard_map(
        body,
        mesh=mesh,
        in_specs=placed,
        out_specs=(P(None, "gz", "gx", None), P(("gx", "gz"), None, None)),
        check_vma=False,
    )
```

profile of v0, /device:TPU:1, one launch (start us, length us, event | category | flops | bytes accessed | tf_op | source)
XLA Modules:
  0.0 297.4 jit_solution(10143383695126811116)
XLA Ops:
  0.6 1.3 collective-permute-start
  1.9 4.9 %collective-permute-start.1 = (bf16[16,1,64,2048]{3,2,1,0:T(8,128)(2,1)}, bf16[16,1,64,2048]{3,2,1,0:T(8,128)(2,1)S(1)}, u32[]{:S(2)}, u32[]{:S(2)}) collective-permute-start(bf16[16,1,64,2048]{3,2,1,0:T(8,128)(2,1)} %param.9), channel_id=1, source_target_pairs={{0,1},{1,2},{2,3},{4,5},{5,6},{6,7},{8,9},{9,10},{10,11},{12,13},{... | collective-permute-start | bytes 12582920 | tf_op jit(solution)/shard_map/ppermute | solution.py:17
  6.9 87.9 %collective-permute-done = bf16[16,1,64,2048]{3,2,1,0:T(8,128)(2,1)S(1)} collective-permute-done((bf16[16,1,64,2048]{3,2,1,0:T(8,128)(2,1)}, bf16[16,1,64,2048]{3,2,1,0:T(8,128)(2,1)S(1)}, u32[]{:S(2)}, u32[]{:S(2)}) %collective-permute-start) | collective-permute-done | bytes 4194336 | tf_op jit(solution)/shard_map/ppermute | solution.py:19
  94.8 1.0 collective-permute-done.1
  95.7 14.3 %convert_bitcast_fusion = bf16[16,1,64,2048]{3,2,0,1:T(8,128)(2,1)} fusion(bf16[1,2048,2048]{2,1,0:T(8,128)(2,1)} %param.11, bf16[16,1,64,2048]{3,2,1,0:T(8,128)(2,1)S(1)} %collective-permute-done.1, bf16[16,1,64,2048]{3,2,1,0:T(8,128)(2,1)S(1)} %collective-permute-done, bf16[16,1,64,2048]{3,2,1,0:T(8,128)(2,1)} %param.9, f32[64,2048]{1,0:T(8,128)} %bitcast.66), kind=kOutput, calls=%fused_computation.12 | convolution fusion | flops 8610906112 | bytes 25690112 | tf_op jit(solution)/shard_map/tzyj,zij->tzyi/dot_general | solution.py:34
  110.0 10.9 %copy.18 = bf16[16,1,64,2048]{2,0,1,3:T(8,128)(2,1)} copy(bf16[16,1,64,2048]{3,2,0,1:T(8,128)(2,1)} %convert_bitcast_fusion) | data formatting | bytes 8388608 | tf_op jit(solution)/shard_map/convert_element_type | solution.py:36
  121.0 13.9 %reshape.59 = bf16[32,2,32768]{2,1,0:T(2,128)(2,1)} reshape(bf16[2048,1,16,64]{3,2,1,0:T(8,128)(2,1)} %bitcast.59) | data formatting | bytes 8388608
  134.8 0.0 copy-start
  134.8 0.0 copy-start.2
  134.8 0.0 copy-start.3
  134.8 10.2 %all-to-all-start = ((bf16[32,2,32768]{2,1,0:T(2,128)(2,1)}), bf16[32,2,32768]{2,1,0:T(2,128)(2,1)}, u32[]{:S(2)}, u32[]{:S(2)}) async-start(bf16[32,2,32768]{2,1,0:T(2,128)(2,1)} %reshape.59), calls=%async_computation | async-start | bytes 8388608 | tf_op jit(solution)/shard_map/all_to_all | solution.py:39
  145.7 0.0 copy-done
  145.8 0.1 copy.21
  145.9 0.0 copy-done.2
  145.9 0.0 copy-done.3
  145.9 49.3 %all-to-all-done = bf16[32,2,32768]{2,1,0:T(2,128)(2,1)} async-done(((bf16[32,2,32768]{2,1,0:T(2,128)(2,1)}), bf16[32,2,32768]{2,1,0:T(2,128)(2,1)}, u32[]{:S(2)}, u32[]{:S(2)}) %all-to-all-start) | async-done | bytes 4194336 | tf_op jit(solution)/shard_map/all_to_all | solution.py:39
  195.2 13.7 %reshape.60 = bf16[2048,1,16,64]{3,2,1,0:T(8,128)(2,1)} reshape(bf16[32,2,32768]{2,1,0:T(2,128)(2,1)} %all-to-all-done) | data formatting | bytes 8388608
  208.9 12.0 %copy.30 = bf16[16,1,64,32,64]{2,3,4,0,1:T(8,128)(2,1)} copy(bf16[16,1,64,32,64]{2,0,4,3,1:T(8,128)(2,1)} %bitcast.60) | data formatting | bytes 8388608 | tf_op jit(solution)/shard_map/all_to_all | solution.py:39
  220.9 12.3 %reshape.43 = bf16[16,2048,64]{1,2,0:T(8,128)(2,1)} reshape(bf16[16,1,32,64,64]{3,2,4,0,1:T(8,128)(2,1)} %bitcast.61) | data formatting | bytes 8388608 | tf_op jit(solution)/shard_map/reshape.9
  233.2 13.9 %fusion.15 = bf16[16,64,2048]{2,1,0:T(8,128)(2,1)} fusion(bf16[16,2048,64]{1,2,0:T(8,128)(2,1)} %reshape.43, bf16[1,2048,2048]{2,1,0:T(8,128)(2,1)} %param.12), kind=kOutput, calls=%fused_computation.15 | convolution fusion | flops 8592031744 | bytes 16777216 | tf_op jit(solution)/shard_map/tzjx,zij->tzxi/dot_general | solution.py:37
  247.1 7.4 %reshape.45 = bf16[16,1024,128]{2,1,0:T(8,128)(2,1)} reshape(bf16[16,1,64,2048]{3,2,0,1:T(8,128)(2,1)} %bitcast.62) | data formatting | bytes 8388608 | tf_op jit(solution)/shard_map/reshape | solution.py:47
  254.5 6.9 %copy.20 = bf16[16,1024,128]{2,0,1:T(8,128)(2,1)} copy(bf16[16,1024,128]{2,1,0:T(8,128)(2,1)} %reshape.45) | data formatting | bytes 8388608 | tf_op jit(solution)/shard_map/reshape | solution.py:47
  261.3 0.0 copy-start.1
  261.3 3.0 %gather_fusion = bf16[256,16,128]{2,1,0:T(8,128)(2,1)S(1)} fusion(bf16[16,1024,128]{2,0,1:T(8,128)(2,1)} %copy.20, s32[1024]{0:T(1024)S(1)} %pad_clamp_fusion), kind=kCustom, calls=%fused_computation | custom fusion | bytes 2098176 | tf_op jit(solution)/shard_map/jit(_take)/gather | solution.py:49
  264.4 1.3 bitcast_multiply_fusion
  265.7 0.0 copy-done.1
  265.7 1.8 fusion.20
  267.6 0.6 copy.23
  268.2 28.5 %all_to_all.20 = f32[128,1,16,128]{3,2,1,0:T(8,128)S(1)} all-to-all(f32[128,1,16,128]{3,2,1,0:T(8,128)S(1)} %copy.23), channel_id=1, replica_groups=mesh['gx'=32,'gz'=4] {'gx','gz'}, dimensions={0} | all-to-all | bytes 2097152 | tf_op jit(solution)/shard_map/all_to_all | solution.py:63
  296.7 0.7 reduce_sum.9
  (4 shorter events, 0.0 us)
Async XLA Ops:
  0.6 94.1 %collective-permute-start = (bf16[16,1,64,2048]{3,2,1,0:T(8,128)(2,1)}, bf16[16,1,64,2048]{3,2,1,0:T(8,128)(2,1)S(1)}, u32[]{:S(2)}, u32[]{:S(2)}) collective-permute-start(bf16[16,1,64,2048]{3,2,1,0:T(8,128)(2,1)} %param.9), channel_id=1, source_target_pairs={{1,0},{2,1},{3,2},{5,4},{6,5},{7,6},{9,8},{10,9},{11,10},{13,12},{... | collective-permute-start | bytes 12582920 | tf_op jit(solution)/shard_map/ppermute | solution.py:19
  1.9 93.8 %collective-permute-start.1 = (bf16[16,1,64,2048]{3,2,1,0:T(8,128)(2,1)}, bf16[16,1,64,2048]{3,2,1,0:T(8,128)(2,1)S(1)}, u32[]{:S(2)}, u32[]{:S(2)}) collective-permute-start(bf16[16,1,64,2048]{3,2,1,0:T(8,128)(2,1)} %param.9), channel_id=1, source_target_pairs={{0,1},{1,2},{2,3},{4,5},{5,6},{6,7},{8,9},{9,10},{10,11},{12,13},{... | collective-permute-start | bytes 12582920 | tf_op jit(solution)/shard_map/ppermute | solution.py:17
  134.8 10.9 %copy-start = (f32[256,16]{0,1:T(8,128)S(1)}, f32[256,16]{0,1:T(8,128)}, u32[]{:S(2)}) copy-start(f32[256,16]{0,1:T(8,128)} %param.13) | copy-start | bytes 49156
  134.8 11.0 %copy-start.2 = (s32[256]{0:T(256)S(1)}, s32[256]{0:T(256)}, u32[]{:S(2)}) copy-start(s32[256]{0:T(256)} %param.17) | copy-start | bytes 3076
  134.8 11.0 %copy-start.3 = (s32[256]{0:T(256)S(1)}, s32[256]{0:T(256)}, u32[]{:S(2)}) copy-start(s32[256]{0:T(256)} %param.16) | copy-start | bytes 3076
  134.8 60.4 %all-to-all-start = ((bf16[32,2,32768]{2,1,0:T(2,128)(2,1)}), bf16[32,2,32768]{2,1,0:T(2,128)(2,1)}, u32[]{:S(2)}, u32[]{:S(2)}) async-start(bf16[32,2,32768]{2,1,0:T(2,128)(2,1)} %reshape.59), calls=%async_computation | async-start | bytes 8388608 | tf_op jit(solution)/shard_map/all_to_all | solution.py:39
  261.3 4.4 %copy-start.1 = (s32[256,1]{0,1:T(1,128)S(1)}, s32[256,1]{0,1:T(1,128)}, u32[]{:S(2)}) copy-start(s32[256,1]{0,1:T(1,128)} %param.14) | copy-start | bytes 3076
where the time goes:
time: 299 us; the launch traced here: 297 us
  waiting for transfers between devices  138 us (46%)
  local copies, waits for them, and re-layouts  80.8 us (27%)
  matrix products  30 us (10%)
  blocking collectives  28.5 us (10%)
  starting transfers between devices  16.5 us (6%)
    ppermute x1, waiting for transfers between devices, padded_2(): lax.ppermute(head, axis, [((i + 1) % count, i) for i in range(ends)])  87.9 us
    all_to_all x1, waiting for transfers between devices, body(): lax.all_to_all(x_swept, 'gx', split_axis=3, concat_axis=2, tiled=True)  49.3 us
    all_to_all x1, blocking collectives, body(): lax.all_to_all(buffer, ('gx', 'gz'), split_axis=0, concat_axis=0, tiled=T...  28.5 us
    unnamed x10, local copies, waits for them, and re-layouts  27.6 us
    dot_general x1, matrix products, body(): jnp.einsum('tzyj,zij->tzyi', vertical, x_inverse, preferred_element_type=...  14.3 us
    reshape x2, local copies, waits for them, and re-layouts, body(): blocks = adjoint.reshape(test_count, x_local * segments, SEG)  14.2 us
    dot_general x1, matrix products, body(): jnp.einsum('tzjx,zij->tzxi', lax.all_to_all(x_swept, 'gx', split_axis=3,...  13.9 us
    another operation x1, local copies, waits for them, and re-layouts  12.3 us
  transfers between devices with their start and end apart: 3, of which 3 were waited for; matrix products, arithmetic and copies ran while one was open for 0% of the time, Pallas kernels for 0%

commit v1 on v0

v1 whole, which is shorter than its diff:
```python
import functools

import jax
import jax.numpy as jnp
from jax import lax
from jax.experimental import pallas as pl
from jax.experimental.pallas import tpu as pltpu
from jax.sharding import PartitionSpec as P

SEG = 128
CHUNKS = (2, 2, 2, 2)
BLOCK = 512
LIMIT = 52
NT = (((1,), (1,)), ((), ()))
MIB = 1 << 20
ANY = pl.BlockSpec(memory_space=pl.ANY)
VMEM = pl.BlockSpec(memory_space=pltpu.VMEM)
SMEM = pl.BlockSpec(memory_space=pltpu.SMEM)


def params(mib):
    return pltpu.CompilerParams(vmem_limit_bytes=mib * MIB)


def cost(flops, nbytes):
    return pl.CostEstimate(flops=flops, bytes_accessed=nbytes, transcendentals=0)


def fetch(source, buffer, sem):
    copy = pltpu.make_async_copy(source, buffer, sem)
    copy.start()
    return copy


def split_kernel(first, heads, out, sem):
    fetch(heads.at[pl.ds(first, out.shape[0])], out, sem).wait()


def split(heads, first, size):
    return pl.pallas_call(
        functools.partial(split_kernel, first),
        in_specs=[ANY],
        out_specs=ANY,
        out_shape=jax.ShapeDtypeStruct((size,) + heads.shape[1:], heads.dtype),
        scratch_shapes=[pltpu.SemaphoreType.DMA],
        compiler_params=params(LIMIT),
        cost_estimate=cost(0, 2 * MIB),
        name="split",
    )(heads)


def prepare_kernel(gz_count, x_local, count, misfit, owner, cells, hot, *weights):
    rows = owner.shape[1]
    lanes = lax.broadcasted_iota(jnp.int32, hot.shape, 1)
    hot[...] = (cells[...] == lanes).astype(jnp.float32).astype(jnp.bfloat16)

    m = weights[0].shape[1] // 2
    line = lax.broadcasted_iota(jnp.int32, (m, 2 * rows), 0)
    lane = lax.broadcasted_iota(jnp.int32, (m, 2 * rows), 1)
    test = (line // gz_count) % 2
    device = (line // (2 * gz_count)) * gz_count + line % gz_count
    owners = jnp.concatenate([owner[...], owner[...]], axis=1)
    keep = (owners == device) & (lane // rows == test) & (lane % rows < count[0])
    pair = 0
    for out in weights:
        for p in range(out.shape[0]):
            full = jnp.where(keep, misfit[pair : pair + 1], 0.0)
            high = full.astype(jnp.bfloat16)
            out[p, :m] = high
            out[p, m:] = (full - high.astype(jnp.float32)).astype(jnp.bfloat16)
            pair += 1


def prepare(misfit, row_owner, row_count, row_x, row_seg, x_local, segments, gx_count, gz_count):
    rows, tests = misfit.shape
    m = 2 * gx_count * gz_count
    cell = (row_seg * x_local + row_x).reshape(rows, 1)
    return pl.pallas_call(
        functools.partial(prepare_kernel, gz_count, x_local),
        in_specs=[SMEM, VMEM, VMEM, VMEM],
        out_specs=[VMEM] * (1 + len(CHUNKS)),
        out_shape=[jax.ShapeDtypeStruct((rows, x_local * segments), jnp.bfloat16)]
        + [jax.ShapeDtypeStruct((size, 2 * m, 2 * rows), jnp.bfloat16) for size in CHUNKS],
        compiler_params=params(40),
        cost_estimate=cost(0, 6 * MIB),
        name="prepare",
    )(row_count, misfit.T.reshape(tests // 2, 2 * rows), row_owner.T, cell)


def x_kernel(
    first, own, above, below, leak, inverse, after, out,
    own_v, above_v, below_v, leak_v, inverse_v, vertical, staged, sems, block_sems, out_sems,
):
    tests, _, lines, _ = own_v.shape
    inputs = [
        fetch(source, buffer, sems.at[i])
        for i, (source, buffer) in enumerate(
            [
                (leak, leak_v),
                (own.at[pl.ds(first, tests)], own_v),
                (above, above_v),
                (below, below_v),
            ]
        )
    ]
    cells = staged.shape[0]
    blocks = [
        fetch(
            inverse.at[:, pl.ds(k, BLOCK)], inverse_v.at[:, pl.ds(k, BLOCK)], block_sems.at[k // BLOCK]
        )
        for k in range(0, cells, BLOCK)
    ]
    for copy in inputs:
        copy.wait()
    for t in range(tests):
        centre = own_v[t, 0].astype(jnp.float32)
        near = above_v[t, 0].astype(jnp.float32) + below_v[t, 0].astype(jnp.float32)
        vertical[t * lines : (t + 1) * lines] = (
            centre + leak_v[0] * (near - 2.0 * centre)
        ).astype(jnp.bfloat16)
    sent = []
    for k in range(0, cells, BLOCK):
        blocks[k // BLOCK].wait()
        swept = lax.dot_general(
            vertical[...], inverse_v[0, k : k + BLOCK], NT, preferred_element_type=jnp.float32
        ).astype(jnp.bfloat16)
        staged[k : k + BLOCK] = swept.T
        sent.append(
            fetch(staged.at[pl.ds(k, BLOCK)], out.at[pl.ds(k, BLOCK)], out_sems.at[k // BLOCK])
        )
    for copy in sent:
        copy.wait()


def x_sweep(own, first, above, below, leak, inverse, after):
    tests, _, lines, width = above.shape
    cells = inverse.shape[1]
    part = pltpu.VMEM(above.shape, above.dtype)
    return pl.pallas_call(
        functools.partial(x_kernel, first),
        in_specs=[ANY] * 6,
        out_specs=ANY,
        out_shape=jax.ShapeDtypeStruct((cells, tests * lines), jnp.bfloat16),
        scratch_shapes=[
            part,
            part,
            part,
            pltpu.VMEM(leak.shape, leak.dtype),
            pltpu.VMEM(inverse.shape, inverse.dtype),
            pltpu.VMEM((tests * lines, width), jnp.bfloat16),
            pltpu.VMEM((cells, tests * lines), jnp.bfloat16),
            pltpu.SemaphoreType.DMA((4,)),
            pltpu.SemaphoreType.DMA((cells // BLOCK,)),
            pltpu.SemaphoreType.DMA((cells // BLOCK,)),
        ],
        compiler_params=params(LIMIT),
        cost_estimate=cost(2 * cells * tests * lines * width, 20 * MIB),
        name="x_sweep",
    )(own, above, below, leak, inverse, after)


def y_kernel(first, earlier, swept, inverse, hot, weights, *rest):
    befores = rest[:earlier]
    out, partial, swept_v, inverse_v, hot_v, weights_v, lines, staged, picked, sems, block_sems, out_sems = rest[-12:]
    inputs = [
        fetch(source, buffer, sems.at[i])
        for i, (source, buffer) in enumerate(
            [(swept, swept_v), (hot, hot_v), (weights, weights_v)]
        )
    ]
    sources, x_local, lanes = swept_v.shape
    pairs = lanes // SEG
    tests = 2 * pairs
    y_local = SEG // 2
    cells = inverse_v.shape[1]
    blocks = [
        fetch(
            inverse.at[:, pl.ds(k, BLOCK)], inverse_v.at[:, pl.ds(k, BLOCK)], block_sems.at[k // BLOCK]
        )
        for k in range(0, cells, BLOCK)
    ]

    group = weights_v.shape[1] // 2 // sources
    place = 0
    for before in befores:
        partial[:, place : place + before.shape[1]] = before[...]
        place += before.shape[1]

    inputs[0].wait()
    for p in range(pairs):
        for s in range(sources // 2):
            a = swept_v[2 * s, :, p * SEG : (p + 1) * SEG]
            b = swept_v[2 * s + 1, :, p * SEG : (p + 1) * SEG]
            for t in range(2):
                cut = slice(t * y_local, (t + 1) * y_local)
                lines[
                    (2 * p + t) * x_local : (2 * p + t + 1) * x_local,
                    s * SEG : (s + 1) * SEG,
                ] = jnp.concatenate([a[:, cut], b[:, cut]], axis=1)

    sent = []
    for k in range(0, cells, BLOCK):
        blocks[k // BLOCK].wait()
        done = lax.dot_general(
            lines[...], inverse_v[0, k : k + BLOCK], NT, preferred_element_type=jnp.float32
        ).astype(jnp.bfloat16)
        for t in range(tests):
            staged[t, 0, :, k : k + BLOCK] = done[t * x_local : (t + 1) * x_local]
        sent.append(
            fetch(
                staged.at[:, :, :, pl.ds(k, BLOCK)],
                out.at[pl.ds(first, tests), :, :, pl.ds(k, BLOCK)],
                out_sems.at[k // BLOCK],
            )
        )
        if k == 0:
            inputs[1].wait()
        first_cell = k // SEG * x_local
        for p in range(pairs):
            stack = []
            for s in range(0, BLOCK, SEG):
                stack.append(
                    jnp.concatenate(
                        [
                            done[(2 * p + t) * x_local : (2 * p + t + 1) * x_local, s : s + SEG]
                            for t in range(2)
                        ],
                        axis=1,
                    )
                )
            stack = jnp.concatenate(stack, axis=0)
            found = jnp.dot(
                hot_v[:, first_cell : first_cell + stack.shape[0]],
                stack,
                preferred_element_type=jnp.float32,
            )
            if k == 0:
                picked[p] = found
            else:
                picked[p] += found

    inputs[2].wait()
    for p in range(pairs):
        rows = picked[p].astype(jnp.bfloat16)
        both = jnp.dot(
            weights_v[p],
            jnp.concatenate([rows[:, :SEG], rows[:, SEG:]], axis=0),
            preferred_element_type=jnp.float32,
        )
        half = both.shape[0] // 2
        partial[:, place + p * group : place + (p + 1) * group] = (
            (both[:half] + both[half:])
            .reshape(partial.shape[0], group, SEG)
            .astype(jnp.bfloat16)
        )
    for copy in sent:
        copy.wait()


def y_sweep(swept, inverse, hot, weights, adjoint, befores, first, tests_total):
    sources, x_local, lanes = swept.shape
    pairs = lanes // SEG
    tests = 2 * pairs
    cells = inverse.shape[1]
    rows = hot.shape[0]
    group = weights.shape[1] // 2 // sources
    height = pairs * group + sum(before.shape[1] for before in befores)
    operands = [swept, inverse, hot, weights, *befores]
    in_specs = [ANY] * 4 + [VMEM] * len(befores)
    aliases = {}
    if adjoint is not None:
        aliases = {len(operands): 0}
        operands.append(adjoint)
        in_specs.append(ANY)
    return pl.pallas_call(
        functools.partial(y_kernel, first, len(befores)),
        in_specs=in_specs,
        out_specs=[ANY, VMEM],
        out_shape=[
            jax.ShapeDtypeStruct((tests_total, 1, x_local, cells), jnp.bfloat16),
            jax.ShapeDtypeStruct((sources, height, SEG), jnp.bfloat16),
        ],
        scratch_shapes=[
            pltpu.VMEM(swept.shape, swept.dtype),
            pltpu.VMEM(inverse.shape, inverse.dtype),
            pltpu.VMEM(hot.shape, hot.dtype),
            pltpu.VMEM(weights.shape, weights.dtype),
            pltpu.VMEM((tests * x_local, cells), jnp.bfloat16),
            pltpu.VMEM((tests, 1, x_local, cells), jnp.bfloat16),
            pltpu.VMEM((pairs, rows, 2 * SEG), jnp.float32),
            pltpu.SemaphoreType.DMA((3,)),
            pltpu.SemaphoreType.DMA((cells // BLOCK,)),
            pltpu.SemaphoreType.DMA((cells // BLOCK,)),
        ],
        input_output_aliases=aliases,
        compiler_params=params(LIMIT),
        cost_estimate=cost(2 * cells * tests * x_local * cells, 20 * MIB),
        name="y_sweep",
    )(*operands)


def body(heads, leak, x_inverse, y_inverse, misfit, row_owner, row_count, row_x, row_seg):
    tests, _, y_local, nx = heads.shape
    gx_count = lax.axis_size("gx")
    gz_count = lax.axis_size("gz")
    x_local = nx // gx_count
    ny = y_inverse.shape[1]
    ends = gz_count - 1
    up = [(i, i + 1) for i in range(ends)]
    down = [(i + 1, i) for i in range(ends)]

    spans = [(2 * sum(CHUNKS[:c]), 2 * size) for c, size in enumerate(CHUNKS)]
    arrived = []
    for first, size in spans:
        part = split(heads, first, size)
        arrived.append((lax.ppermute(part, "gz", down), lax.ppermute(part, "gz", up)))

    hot, *weights = prepare(
        misfit, row_owner, row_count, row_x, row_seg, x_local, ny // SEG, gx_count, gz_count
    )

    adjoint = None
    order = [hot, hot]
    partials = []
    for c, (first, size) in enumerate(spans):
        swept = x_sweep(heads, first, *arrived[c], leak, x_inverse, order[c])
        swept = swept.reshape(gx_count, x_local, size * y_local)
        swept = lax.all_to_all(swept, "gx", split_axis=0, concat_axis=0, tiled=True)
        befores = partials if c == len(spans) - 1 else []
        adjoint, partial = y_sweep(
            swept, y_inverse, hot, weights[c], adjoint, befores, first, tests
        )
        partials.append(partial)
        order.append(partial)

    sent = partials[-1].reshape(gx_count, tests, gz_count, SEG)
    sent = jnp.transpose(sent, (0, 2, 1, 3)).reshape(gx_count * gz_count, tests, SEG)
    got = lax.all_to_all(sent, ("gx", "gz"), split_axis=0, concat_axis=0, tiled=True)
    return (adjoint, jnp.sum(got.astype(jnp.float32), axis=0)[None])


def solution(mesh):
    placed = (
        P(None, "gz", "gx", None),
        P("gz", "gx", None),
        P("gz", None, None),
        P("gz", None, None),
        P(("gx", "gz"), None),
        P(("gx", "gz"), None),
        P(("gx", "gz")),
        P(("gx", "gz")),
        P(("gx", "gz")),
    )
    return jax.shard_map(
        body,
        mesh=mesh,
        in_specs=placed,
        out_specs=(P(None, "gz", "gx", None), P(("gx", "gz"), None, None)),
        check_vma=False,
    )
```

time: 299 us -> 236 us (0.79)
  Pallas kernels: 0 us -> 128 us
  waiting for transfers between devices: 138 us -> 20.5 us
  local copies, waits for them, and re-layouts: 80.8 us -> 5.12 us
  starting transfers between devices: 16.5 us -> 58.8 us
  matrix products: 30 us -> 0 us
  blocking collectives: 28.5 us -> 20 us
    pallas_call x0 -> x13, Pallas kernels: none -> 128 us  [the longest x4 68.3 us: split(): pl.pallas_call(functools.partial(split_kernel, first), in_specs=[ANY], ou...]
    ppermute x2 -> x8, waiting for transfers between devices: 88.9 us -> 6.57 us  [the longest x4 5.81 us: body(): lax.ppermute(part, 'gz', down)]
    all_to_all x1 -> x4, waiting for transfers between devices: 49.3 us -> 13.9 us  [body(): swept = lax.all_to_all(swept, 'gx', split_axis=0, concat_axis=0, tiled=True)]
    dot_general x3 -> x0, matrix products: 30 us -> none  [the longest x1 14.3 us: body(): jnp.einsum('tzyj,zij->tzyi', vertical, x_inverse, preferred_element_type=...]
    unnamed x10 -> x20, local copies, waits for them, and re-layouts: 27.6 us -> 4.89 us
    all_to_all x1 -> x4, starting transfers between devices: 10.2 us -> 32 us  [body(): swept = lax.all_to_all(swept, 'gx', split_axis=0, concat_axis=0, tiled=True)]
    ppermute x2 -> x8, starting transfers between devices: 6.22 us -> 26.8 us  [the longest x4 21.6 us: body(): lax.ppermute(part, 'gz', up)]
    reshape x3, local copies, waits for them, and re-layouts: 14.8 us -> 0.23 us  [the longest x1 0.14 us: prepare(): cell = (row_seg * x_local + row_x).reshape(rows, 1)]
  transfers between devices with their start and end apart: 3 -> 12, of which waited for: 3 -> 4; matrix products, arithmetic and copies ran while one was open for 0% -> 0% of each run, Pallas kernels for 0% -> 52%
where the time goes in v1:
time: 236 us; the launch traced here: 235 us
  Pallas kernels  128 us (54%)
  starting transfers between devices  58.8 us (25%)
  waiting for transfers between devices  20.5 us (9%)
  blocking collectives  20 us (8%)
  local copies, waits for them, and re-layouts  5.12 us (2%)
    pallas_call x4, Pallas kernels, split(): pl.pallas_call(functools.partial(split_kernel, first), in_specs=[ANY], ou...  68.3 us
    pallas_call x4, Pallas kernels, x_sweep(): pl.pallas_call(functools.partial(x_kernel, first), in_specs=[ANY] * 6, ou...  35.4 us
    all_to_all x4, starting transfers between devices, body(): swept = lax.all_to_all(swept, 'gx', split_axis=0, concat_axis=0, tiled=True)  32 us
    pallas_call x4, Pallas kernels, y_sweep(): pl.pallas_call(functools.partial(y_kernel, first, len(befores)), in_specs...  23.3 us
    ppermute x4, starting transfers between devices, body(): lax.ppermute(part, 'gz', up)  21.6 us
    all_to_all x1, blocking collectives, body(): lax.all_to_all(sent, ('gx', 'gz'), split_axis=0, concat_axis=0, tiled=True)  20 us
    all_to_all x4, waiting for transfers between devices, body(): swept = lax.all_to_all(swept, 'gx', split_axis=0, concat_axis=0, tiled=True)  13.9 us
    ppermute x4, waiting for transfers between devices, body(): lax.ppermute(part, 'gz', down)  5.81 us
  transfers between devices with their start and end apart: 12, of which 4 were waited for; matrix products, arithmetic and copies ran while one was open for 0% of the time, Pallas kernels for 52%

profile of v1, /device:TPU:1, one launch (start us, length us, event | category | flops | bytes accessed | tf_op | source)
XLA Modules:
  0.0 235.2 jit_solution(6310901870465282627)
XLA Ops:
  0.6 0.0 copy-start.8
  0.7 1.3 split.6
  2.0 1.3 collective-permute-start.4
  3.3 5.8 %collective-permute-start.5 = (bf16[4,1,64,2048]{3,2,1,0:T(8,128)(2,1)S(1)}, bf16[4,1,64,2048]{3,2,1,0:T(8,128)(2,1)}, u32[]{:S(2)}, u32[]{:S(2)}) collective-permute-start(bf16[4,1,64,2048]{3,2,1,0:T(8,128)(2,1)S(1)} %split.6), channel_id=1, source_target_pairs={{0,1},{1,2},{2,3},{4,5},{5,6},{6,7},{8,9},{9,10},{10,11},{12,13},{... | collective-permute-start | bytes 3145736 | tf_op jit(solution)/shard_map/ppermute | solution.py:316
  9.0 1.2 split.5
  10.3 1.3 collective-permute-start.2
  11.6 5.0 %collective-permute-start.3 = (bf16[4,1,64,2048]{3,2,1,0:T(8,128)(2,1)S(1)}, bf16[4,1,64,2048]{3,2,1,0:T(8,128)(2,1)}, u32[]{:S(2)}, u32[]{:S(2)}) collective-permute-start(bf16[4,1,64,2048]{3,2,1,0:T(8,128)(2,1)S(1)} %split.5), channel_id=1, source_target_pairs={{0,1},{1,2},{2,3},{4,5},{5,6},{6,7},{8,9},{9,10},{10,11},{12,13},{... | collective-permute-start | bytes 3145736 | tf_op jit(solution)/shard_map/ppermute | solution.py:316
  16.6 0.0 copy-done.9
  16.6 0.1 copy.14.cells
  17.4 1.5 prepare.1
  18.9 1.0 copy-done.1
  19.8 1.0 copy-done.2
  20.9 1.0 copy-done.3
  21.8 1.0 copy-done.4
  22.8 5.8 %collective-permute-done.4.above = bf16[4,1,64,2048]{3,2,1,0:T(8,128)(2,1)} collective-permute-done((bf16[4,1,64,2048]{3,2,1,0:T(8,128)(2,1)S(1)}, bf16[4,1,64,2048]{3,2,1,0:T(8,128)(2,1)}, u32[]{:S(2)}, u32[]{:S(2)}) %collective-permute-start.4) | collective-permute-done | bytes 1048608 | tf_op jit(solution)/shard_map/ppermute | solution.py:316
  28.6 0.8 collective-permute-done.5.below
  29.4 8.9 %x_sweep.5 = bf16[2048,256]{1,0:T(8,128)(2,1)} custom-call(bf16[16,1,64,2048]{3,2,1,0:T(8,128)(2,1)} %own.7, bf16[4,1,64,2048]{3,2,1,0:T(8,128)(2,1)} %collective-permute-done.4.above, bf16[4,1,64,2048]{3,2,1,0:T(8,128)(2,1)} %collective-permute-done.5.below, f32[1,64,2048]{2,1,0:T(8,128)S(1)} %copy-done, bf16[1,2048,2048]{2,1,0:T(8,128)(2,1)} %inverse.13, ...), custom_call_target="tpu_custom_call" | custom-call | flops 2147483648 | bytes 20971520 | tf_op jit(solution)/shard_map/x_sweep/pallas_call | solution.py:139
  38.2 11.5 %all-to-all-start.1 = ((bf16[32,64,256]{2,1,0:T(8,128)(2,1)}), bf16[32,64,256]{2,1,0:T(8,128)(2,1)S(1)}, u32[]{:S(2)}, u32[]{:S(2)}) async-start(bf16[32,64,256]{2,1,0:T(8,128)(2,1)} %bitcast.15), calls=%async_computation.1 | async-start | bytes 2097152 | tf_op jit(solution)/shard_map/all_to_all | solution.py:328
  49.7 32.9 %split.7 = bf16[4,1,64,2048]{3,2,1,0:T(8,128)(2,1)} custom-call(bf16[16,1,64,2048]{3,2,1,0:T(8,128)(2,1)} %own.7), custom_call_target="tpu_custom_call" | custom-call | bytes 2097152 | tf_op jit(solution)/shard_map/split/pallas_call | solution.py:40
  82.6 1.3 collective-permute-start.6
  83.9 5.9 %collective-permute-start.7 = (bf16[4,1,64,2048]{3,2,1,0:T(8,128)(2,1)}, bf16[4,1,64,2048]{3,2,1,0:T(8,128)(2,1)}, u32[]{:S(2)}, u32[]{:S(2)}) collective-permute-start(bf16[4,1,64,2048]{3,2,1,0:T(8,128)(2,1)} %split.7), channel_id=1, source_target_pairs={{0,1},{1,2},{2,3},{4,5},{5,6},{6,7},{8,9},{9,10},{10,11},{12,13},{... | collective-permute-start | bytes 3145736 | tf_op jit(solution)/shard_map/ppermute | solution.py:316
  89.8 0.0 collective-permute-done.2.above
  89.8 0.0 collective-permute-done.3.below
  89.8 8.8 %x_sweep.4 = bf16[2048,256]{1,0:T(8,128)(2,1)} custom-call(bf16[16,1,64,2048]{3,2,1,0:T(8,128)(2,1)} %own.7, bf16[4,1,64,2048]{3,2,1,0:T(8,128)(2,1)} %collective-permute-done.2.above, bf16[4,1,64,2048]{3,2,1,0:T(8,128)(2,1)} %collective-permute-done.3.below, f32[1,64,2048]{2,1,0:T(8,128)S(1)} %copy-done, bf16[1,2048,2048]{2,1,0:T(8,128)(2,1)} %inverse.13, ...), custom_call_target="tpu_custom_call" | custom-call | flops 2147483648 | bytes 20971520 | tf_op jit(solution)/shard_map/x_sweep/pallas_call | solution.py:139
  98.7 0.0 all-to-all-done.1.swept
  98.7 7.7 %all-to-all-start = ((bf16[32,64,256]{2,1,0:T(8,128)(2,1)}), bf16[32,64,256]{2,1,0:T(8,128)(2,1)S(1)}, u32[]{:S(2)}, u32[]{:S(2)}) async-start(bf16[32,64,256]{2,1,0:T(8,128)(2,1)} %bitcast.14), calls=%async_computation | async-start | bytes 2097152 | tf_op jit(solution)/shard_map/all_to_all | solution.py:328
  106.4 32.9 %split.4 = bf16[4,1,64,2048]{3,2,1,0:T(8,128)(2,1)} custom-call(bf16[16,1,64,2048]{3,2,1,0:T(8,128)(2,1)} %own.7), custom_call_target="tpu_custom_call" | custom-call | bytes 2097152 | tf_op jit(solution)/shard_map/split/pallas_call | solution.py:40
  139.3 1.3 collective-permute-start
  140.6 5.0 %collective-permute-start.1 = (bf16[4,1,64,2048]{3,2,1,0:T(8,128)(2,1)}, bf16[4,1,64,2048]{3,2,1,0:T(8,128)(2,1)}, u32[]{:S(2)}, u32[]{:S(2)}) collective-permute-start(bf16[4,1,64,2048]{3,2,1,0:T(8,128)(2,1)} %split.4), channel_id=1, source_target_pairs={{0,1},{1,2},{2,3},{4,5},{5,6},{6,7},{8,9},{9,10},{10,11},{12,13},{... | collective-permute-start | bytes 3145736 | tf_op jit(solution)/shard_map/ppermute | solution.py:316
  145.5 5.8 %y_sweep.4 = (bf16[16,1,64,2048]{3,2,1,0:T(8,128)(2,1)}, bf16[32,16,128]{2,1,0:T(8,128)(2,1)S(1)}) custom-call(bf16[32,64,256]{2,1,0:T(8,128)(2,1)S(1)} %all-to-all-done.1.swept, bf16[1,2048,2048]{2,1,0:T(8,128)(2,1)} %inverse.15, bf16[256,1024]{1,0:T(8,128)(2,1)S(1)} %get-tuple-element.15.after.hot, bf16[2,512,512]{2,1,0:T(8,128)(2,1)} %copy-done.1), custom_call_target="tpu_custom_call" | custom-call | flops 2147483648 | bytes 20971520 | tf_op jit(solution)/shard_map/y_sweep/pallas_call | solution.py:275
  151.3 0.0 collective-permute-done.6.above
  151.3 0.0 collective-permute-done.7.below
  151.3 8.8 %x_sweep.7 = bf16[2048,256]{1,0:T(8,128)(2,1)} custom-call(bf16[16,1,64,2048]{3,2,1,0:T(8,128)(2,1)} %own.7, bf16[4,1,64,2048]{3,2,1,0:T(8,128)(2,1)} %collective-permute-done.6.above, bf16[4,1,64,2048]{3,2,1,0:T(8,128)(2,1)} %collective-permute-done.7.below, f32[1,64,2048]{2,1,0:T(8,128)S(1)} %copy-done, bf16[1,2048,2048]{2,1,0:T(8,128)(2,1)} %inverse.13, ...), custom_call_target="tpu_custom_call" | custom-call | flops 2147483648 | bytes 20971520 | tf_op jit(solution)/shard_map/x_sweep/pallas_call | solution.py:139
  160.2 0.0 all-to-all-done.swept
  160.2 8.0 %all-to-all-start.3 = ((bf16[32,64,256]{2,1,0:T(8,128)(2,1)}), bf16[32,64,256]{2,1,0:T(8,128)(2,1)S(1)}, u32[]{:S(2)}, u32[]{:S(2)}) async-start(bf16[32,64,256]{2,1,0:T(8,128)(2,1)} %bitcast.6), calls=%async_computation.3 | async-start | bytes 2097152 | tf_op jit(solution)/shard_map/all_to_all | solution.py:328
  168.2 5.8 %y_sweep.5 = (bf16[16,1,64,2048]{3,2,1,0:T(8,128)(2,1)}, bf16[32,16,128]{2,1,0:T(8,128)(2,1)S(1)}) custom-call(bf16[32,64,256]{2,1,0:T(8,128)(2,1)S(1)} %all-to-all-done.swept, bf16[1,2048,2048]{2,1,0:T(8,128)(2,1)} %inverse.15, bf16[256,1024]{1,0:T(8,128)(2,1)S(1)} %get-tuple-element.15.after.hot, ...), custom_call_target="tpu_custom_call", output_to_operand_aliasing={{0}: (4, {})} | custom-call | flops 2147483648 | bytes 20971520 | tf_op jit(solution)/shard_map/y_sweep/pallas_call | solution.py:275
  173.9 0.0 collective-permute-done.above
  173.9 0.0 collective-permute-done.1.below
  174.0 8.9 %x_sweep.6 = bf16[2048,256]{1,0:T(8,128)(2,1)} custom-call(bf16[16,1,64,2048]{3,2,1,0:T(8,128)(2,1)} %own.7, bf16[4,1,64,2048]{3,2,1,0:T(8,128)(2,1)} %collective-permute-done.above, bf16[4,1,64,2048]{3,2,1,0:T(8,128)(2,1)} %collective-permute-done.1.below, f32[1,64,2048]{2,1,0:T(8,128)S(1)} %copy-done, bf16[1,2048,2048]{2,1,0:T(8,128)(2,1)} %inverse.13, ...), custom_call_target="tpu_custom_call" | custom-call | flops 2147483648 | bytes 20971520 | tf_op jit(solution)/shard_map/x_sweep/pallas_call | solution.py:139
  182.8 2.5 %all-to-all-done.3.swept = bf16[32,64,256]{2,1,0:T(8,128)(2,1)S(1)} async-done(((bf16[32,64,256]{2,1,0:T(8,128)(2,1)}), bf16[32,64,256]{2,1,0:T(8,128)(2,1)S(1)}, u32[]{:S(2)}, u32[]{:S(2)}) %all-to-all-start.3) | async-done | bytes 1048608 | tf_op jit(solution)/shard_map/all_to_all | solution.py:328
  185.3 4.9 %all-to-all-start.2 = ((bf16[32,64,256]{2,1,0:T(8,128)(2,1)}), bf16[32,64,256]{2,1,0:T(8,128)(2,1)S(1)}, u32[]{:S(2)}, u32[]{:S(2)}) async-start(bf16[32,64,256]{2,1,0:T(8,128)(2,1)} %bitcast.5), calls=%async_computation.2 | async-start | bytes 2097152 | tf_op jit(solution)/shard_map/all_to_all | solution.py:328
  190.2 5.8 %y_sweep.6 = (bf16[16,1,64,2048]{3,2,1,0:T(8,128)(2,1)}, bf16[32,16,128]{2,1,0:T(8,128)(2,1)S(1)}) custom-call(bf16[32,64,256]{2,1,0:T(8,128)(2,1)S(1)} %all-to-all-done.3.swept, bf16[1,2048,2048]{2,1,0:T(8,128)(2,1)} %inverse.15, bf16[256,1024]{1,0:T(8,128)(2,1)S(1)} %get-tuple-element.15.after.hot, ...), custom_call_target="tpu_custom_call", output_to_operand_aliasing={{0}: (4, {})} | custom-call | flops 2147483648 | bytes 20971520 | tf_op jit(solution)/shard_map/y_sweep/pallas_call | solution.py:275
  196.0 11.4 %all-to-all-done.2.swept = bf16[32,64,256]{2,1,0:T(8,128)(2,1)S(1)} async-done(((bf16[32,64,256]{2,1,0:T(8,128)(2,1)}), bf16[32,64,256]{2,1,0:T(8,128)(2,1)S(1)}, u32[]{:S(2)}, u32[]{:S(2)}) %all-to-all-start.2) | async-done | bytes 1048608 | tf_op jit(solution)/shard_map/all_to_all | solution.py:328
  207.4 1.0 copy-done.6
  208.4 6.0 %y_sweep.7 = (bf16[16,1,64,2048]{3,2,1,0:T(8,128)(2,1)}, bf16[32,64,128]{2,1,0:T(8,128)(2,1)S(1)}) custom-call(bf16[32,64,256]{2,1,0:T(8,128)(2,1)} %copy-done.6, bf16[1,2048,2048]{2,1,0:T(8,128)(2,1)} %inverse.15, bf16[256,1024]{1,0:T(8,128)(2,1)S(1)} %get-tuple-element.15.after.hot, ...), custom_call_target="tpu_custom_call", output_to_operand_aliasing={{0}: (7, {})} | custom-call | flops 2147483648 | bytes 20971520 | tf_op jit(solution)/shard_map/y_sweep/pallas_call | solution.py:275
  214.4 0.1 copy.15
  214.5 20.0 %all_to_all.25 = bf16[128,16,128]{2,1,0:T(8,128)(2,1)S(1)} all-to-all(bf16[128,16,128]{2,1,0:T(8,128)(2,1)S(1)} %bitcast.16), channel_id=1, replica_groups=mesh['gx'=32,'gz'=4] {'gx','gz'}, dimensions={0} | all-to-all | bytes 1048576 | tf_op jit(solution)/shard_map/all_to_all | solution.py:338
  234.5 0.7 convert_reduce_fusion
  (15 shorter events, 0.0 us)
Async XLA Ops:
  0.6 15.9 %copy-start.8 = (s32[256]{0:T(256)S(1)}, s32[256]{0:T(256)}, u32[]{:S(2)}) copy-start(s32[256]{0:T(256)} %param.16) | copy-start | bytes 3076
  0.6 15.9 %copy-start.9 = (s32[256]{0:T(256)S(1)}, s32[256]{0:T(256)}, u32[]{:S(2)}) copy-start(s32[256]{0:T(256)} %param.17) | copy-start | bytes 3076
  0.7 16.1 %copy-start.7 = (f32[256,16]{0,1:T(8,128)S(1)}, f32[256,16]{0,1:T(8,128)}, u32[]{:S(2)}) copy-start(f32[256,16]{0,1:T(8,128)} %param.13) | copy-start | bytes 49156
  0.7 16.7 %copy-start.5 = (s32[256,1]{0,1:T(1,128)S(1)}, s32[256,1]{0,1:T(1,128)}, u32[]{:S(2)}) copy-start(s32[256,1]{0,1:T(1,128)} %param.14) | copy-start | bytes 3076
  0.7 28.7 %copy-start = (f32[1,64,2048]{2,1,0:T(8,128)S(1)}, f32[1,64,2048]{2,1,0:T(8,128)}, u32[]{:S(2)}) copy-start(f32[1,64,2048]{2,1,0:T(8,128)} %leak.7) | copy-start | bytes 1572868
  2.0 26.6 %collective-permute-start.4 = (bf16[4,1,64,2048]{3,2,1,0:T(8,128)(2,1)S(1)}, bf16[4,1,64,2048]{3,2,1,0:T(8,128)(2,1)}, u32[]{:S(2)}, u32[]{:S(2)}) collective-permute-start(bf16[4,1,64,2048]{3,2,1,0:T(8,128)(2,1)S(1)} %split.6), channel_id=1, source_target_pairs={{1,0},{2,1},{3,2},{5,4},{6,5},{7,6},{9,8},{10,9},{11,10},{13,12},{... | collective-permute-start | bytes 3145736 | tf_op jit(solution)/shard_map/ppermute | solution.py:316
  3.3 26.1 %collective-permute-start.5 = (bf16[4,1,64,2048]{3,2,1,0:T(8,128)(2,1)S(1)}, bf16[4,1,64,2048]{3,2,1,0:T(8,128)(2,1)}, u32[]{:S(2)}, u32[]{:S(2)}) collective-permute-start(bf16[4,1,64,2048]{3,2,1,0:T(8,128)(2,1)S(1)} %split.6), channel_id=1, source_target_pairs={{0,1},{1,2},{2,3},{4,5},{5,6},{6,7},{8,9},{9,10},{10,11},{12,13},{... | collective-permute-start | bytes 3145736 | tf_op jit(solution)/shard_map/ppermute | solution.py:316
  10.3 79.6 %collective-permute-start.2 = (bf16[4,1,64,2048]{3,2,1,0:T(8,128)(2,1)S(1)}, bf16[4,1,64,2048]{3,2,1,0:T(8,128)(2,1)}, u32[]{:S(2)}, u32[]{:S(2)}) collective-permute-start(bf16[4,1,64,2048]{3,2,1,0:T(8,128)(2,1)S(1)} %split.5), channel_id=1, source_target_pairs={{1,0},{2,1},{3,2},{5,4},{6,5},{7,6},{9,8},{10,9},{11,10},{13,12},{... | collective-permute-start | bytes 3145736 | tf_op jit(solution)/shard_map/ppermute | solution.py:316
  11.6 78.3 %collective-permute-start.3 = (bf16[4,1,64,2048]{3,2,1,0:T(8,128)(2,1)S(1)}, bf16[4,1,64,2048]{3,2,1,0:T(8,128)(2,1)}, u32[]{:S(2)}, u32[]{:S(2)}) collective-permute-start(bf16[4,1,64,2048]{3,2,1,0:T(8,128)(2,1)S(1)} %split.5), channel_id=1, source_target_pairs={{0,1},{1,2},{2,3},{4,5},{5,6},{6,7},{8,9},{9,10},{10,11},{12,13},{... | collective-permute-start | bytes 3145736 | tf_op jit(solution)/shard_map/ppermute | solution.py:316
  18.9 1.0 copy-start.1
  19.8 1.0 copy-start.2
  20.8 1.0 copy-start.3
  21.8 1.0 copy-start.4
  38.2 60.5 %all-to-all-start.1 = ((bf16[32,64,256]{2,1,0:T(8,128)(2,1)}), bf16[32,64,256]{2,1,0:T(8,128)(2,1)S(1)}, u32[]{:S(2)}, u32[]{:S(2)}) async-start(bf16[32,64,256]{2,1,0:T(8,128)(2,1)} %bitcast.15), calls=%async_computation.1 | async-start | bytes 2097152 | tf_op jit(solution)/shard_map/all_to_all | solution.py:328
  82.6 68.7 %collective-permute-start.6 = (bf16[4,1,64,2048]{3,2,1,0:T(8,128)(2,1)}, bf16[4,1,64,2048]{3,2,1,0:T(8,128)(2,1)}, u32[]{:S(2)}, u32[]{:S(2)}) collective-permute-start(bf16[4,1,64,2048]{3,2,1,0:T(8,128)(2,1)} %split.7), channel_id=1, source_target_pairs={{1,0},{2,1},{3,2},{5,4},{6,5},{7,6},{9,8},{10,9},{11,10},{13,12},{... | collective-permute-start | bytes 3145736 | tf_op jit(solution)/shard_map/ppermute | solution.py:316
  83.9 67.4 %collective-permute-start.7 = (bf16[4,1,64,2048]{3,2,1,0:T(8,128)(2,1)}, bf16[4,1,64,2048]{3,2,1,0:T(8,128)(2,1)}, u32[]{:S(2)}, u32[]{:S(2)}) collective-permute-start(bf16[4,1,64,2048]{3,2,1,0:T(8,128)(2,1)} %split.7), channel_id=1, source_target_pairs={{0,1},{1,2},{2,3},{4,5},{5,6},{6,7},{8,9},{9,10},{10,11},{12,13},{... | collective-permute-start | bytes 3145736 | tf_op jit(solution)/shard_map/ppermute | solution.py:316
  98.7 61.5 %all-to-all-start = ((bf16[32,64,256]{2,1,0:T(8,128)(2,1)}), bf16[32,64,256]{2,1,0:T(8,128)(2,1)S(1)}, u32[]{:S(2)}, u32[]{:S(2)}) async-start(bf16[32,64,256]{2,1,0:T(8,128)(2,1)} %bitcast.14), calls=%async_computation | async-start | bytes 2097152 | tf_op jit(solution)/shard_map/all_to_all | solution.py:328
  139.3 34.7 %collective-permute-start = (bf16[4,1,64,2048]{3,2,1,0:T(8,128)(2,1)}, bf16[4,1,64,2048]{3,2,1,0:T(8,128)(2,1)}, u32[]{:S(2)}, u32[]{:S(2)}) collective-permute-start(bf16[4,1,64,2048]{3,2,1,0:T(8,128)(2,1)} %split.4), channel_id=1, source_target_pairs={{1,0},{2,1},{3,2},{5,4},{6,5},{7,6},{9,8},{10,9},{11,10},{13,12},{... | collective-permute-start | bytes 3145736 | tf_op jit(solution)/shard_map/ppermute | solution.py:316
  140.6 33.4 %collective-permute-start.1 = (bf16[4,1,64,2048]{3,2,1,0:T(8,128)(2,1)}, bf16[4,1,64,2048]{3,2,1,0:T(8,128)(2,1)}, u32[]{:S(2)}, u32[]{:S(2)}) collective-permute-start(bf16[4,1,64,2048]{3,2,1,0:T(8,128)(2,1)} %split.4), channel_id=1, source_target_pairs={{0,1},{1,2},{2,3},{4,5},{5,6},{6,7},{8,9},{9,10},{10,11},{12,13},{... | collective-permute-start | bytes 3145736 | tf_op jit(solution)/shard_map/ppermute | solution.py:316
  160.2 25.1 %all-to-all-start.3 = ((bf16[32,64,256]{2,1,0:T(8,128)(2,1)}), bf16[32,64,256]{2,1,0:T(8,128)(2,1)S(1)}, u32[]{:S(2)}, u32[]{:S(2)}) async-start(bf16[32,64,256]{2,1,0:T(8,128)(2,1)} %bitcast.6), calls=%async_computation.3 | async-start | bytes 2097152 | tf_op jit(solution)/shard_map/all_to_all | solution.py:328
  185.3 22.1 %all-to-all-start.2 = ((bf16[32,64,256]{2,1,0:T(8,128)(2,1)}), bf16[32,64,256]{2,1,0:T(8,128)(2,1)S(1)}, u32[]{:S(2)}, u32[]{:S(2)}) async-start(bf16[32,64,256]{2,1,0:T(8,128)(2,1)} %bitcast.5), calls=%async_computation.2 | async-start | bytes 2097152 | tf_op jit(solution)/shard_map/all_to_all | solution.py:328
  207.4 1.0 copy-start.6

commit v2 on v1

--- a/solution.py
+++ b/solution.py
@@ -10,7 +10,11 @@
 SEG = 128
 CHUNKS = (2, 2, 2, 2)
 BLOCK = 512
-LIMIT = 52
+BLOCKS = 4
+X_LIMIT = 52
+Y_LIMIT = 52
+LOAD_LIMIT = 50
+RESIDENT_LIMIT = 44
 NT = (((1,), (1,)), ((), ()))
 MIB = 1 << 20
 ANY = pl.BlockSpec(memory_space=pl.ANY)
@@ -32,24 +36,46 @@
     return copy
 
 
-def split_kernel(first, heads, out, sem):
-    fetch(heads.at[pl.ds(first, out.shape[0])], out, sem).wait()
-
-
-def split(heads, first, size):
+def split_kernel(first, heads, *rest):
+    out, buffer, sems = rest[-3:]
+    fetch(heads.at[pl.ds(first, out.shape[0])], buffer, sems.at[0]).wait()
+    fetch(buffer, out, sems.at[1]).wait()
+
+
+def split(heads, first, size, after=()):
     return pl.pallas_call(
         functools.partial(split_kernel, first),
-        in_specs=[ANY],
+        in_specs=[ANY] * (1 + len(after)),
         out_specs=ANY,
         out_shape=jax.ShapeDtypeStruct((size,) + heads.shape[1:], heads.dtype),
-        scratch_shapes=[pltpu.SemaphoreType.DMA],
-        compiler_params=params(LIMIT),
+        scratch_shapes=[
+            pltpu.VMEM((size,) + heads.shape[1:], heads.dtype),
+            pltpu.SemaphoreType.DMA((2,)),
+        ],
+        compiler_params=params(X_LIMIT),
         cost_estimate=cost(0, 2 * MIB),
         name="split",
-    )(heads)
-
-
-def prepare_kernel(gz_count, x_local, count, misfit, owner, cells, hot, *weights):
+    )(heads, *after)
+
+
+def load_kernel(source, after, out, sem):
+    fetch(source, out, sem).wait()
+
+
+def load(inverse, after):
+    return pl.pallas_call(
+        load_kernel,
+        in_specs=[ANY, ANY],
+        out_specs=VMEM,
+        out_shape=pltpu.VMEM(inverse.shape, inverse.dtype),
+        scratch_shapes=[pltpu.SemaphoreType.DMA],
+        compiler_params=params(LOAD_LIMIT),
+        cost_estimate=cost(0, 16 * MIB),
+        name="load",
+    )(inverse, after)
+
+
+def prepare_kernel(gz_count, count, misfit, owner, cells, after, hot, *weights):
     rows = owner.shape[1]
     lanes = lax.broadcasted_iota(jnp.int32, hot.shape, 1)
     hot[...] = (cells[...] == lanes).astype(jnp.float32).astype(jnp.bfloat16)
@@ -71,74 +97,84 @@
             pair += 1
 
 
-def prepare(misfit, row_owner, row_count, row_x, row_seg, x_local, segments, gx_count, gz_count):
+def prepare(
+    misfit, row_owner, row_count, row_x, row_seg, x_local, segments, gx_count, gz_count, after
+):
     rows, tests = misfit.shape
     m = 2 * gx_count * gz_count
     cell = (row_seg * x_local + row_x).reshape(rows, 1)
     return pl.pallas_call(
-        functools.partial(prepare_kernel, gz_count, x_local),
-        in_specs=[SMEM, VMEM, VMEM, VMEM],
+        functools.partial(prepare_kernel, gz_count),
+        in_specs=[SMEM, VMEM, VMEM, VMEM, ANY],
         out_specs=[VMEM] * (1 + len(CHUNKS)),
         out_shape=[jax.ShapeDtypeStruct((rows, x_local * segments), jnp.bfloat16)]
         + [jax.ShapeDtypeStruct((size, 2 * m, 2 * rows), jnp.bfloat16) for size in CHUNKS],
-        compiler_params=params(40),
+        compiler_params=params(24),
         cost_estimate=cost(0, 6 * MIB),
         name="prepare",
-    )(row_count, misfit.T.reshape(tests // 2, 2 * rows), row_owner.T, cell)
-
-
-def x_kernel(
-    first, own, above, below, leak, inverse, after, out,
-    own_v, above_v, below_v, leak_v, inverse_v, vertical, staged, sems, block_sems, out_sems,
-):
+    )(row_count, misfit.T.reshape(tests // 2, 2 * rows), row_owner.T, cell, after)
+
+
+def x_kernel(first, waits, resident, ends, own, above, below, leak, inverse, *rest):
+    out, own_v, above_v, below_v, leak_v, inverse_v, vertical, staged, sems, block_sems, out_sems = rest[
+        waits:
+    ]
     tests, _, lines, _ = own_v.shape
-    inputs = [
-        fetch(source, buffer, sems.at[i])
-        for i, (source, buffer) in enumerate(
-            [
-                (leak, leak_v),
-                (own.at[pl.ds(first, tests)], own_v),
-                (above, above_v),
-                (below, below_v),
-            ]
-        )
+    cells = staged.shape[0]
+    size = cells // BLOCKS
+    leak_copy = fetch(leak, leak_v, sems.at[3 * tests])
+    parts = [
+        [
+            fetch(own.at[pl.ds(first + t, 1)], own_v.at[pl.ds(t, 1)], sems.at[3 * t]),
+            fetch(above.at[pl.ds(t, 1)], above_v.at[pl.ds(t, 1)], sems.at[3 * t + 1]),
+            fetch(below.at[pl.ds(t, 1)], below_v.at[pl.ds(t, 1)], sems.at[3 * t + 2]),
+        ]
+        for t in range(tests)
     ]
-    cells = staged.shape[0]
-    blocks = [
-        fetch(
-            inverse.at[:, pl.ds(k, BLOCK)], inverse_v.at[:, pl.ds(k, BLOCK)], block_sems.at[k // BLOCK]
-        )
-        for k in range(0, cells, BLOCK)
-    ]
-    for copy in inputs:
-        copy.wait()
+    blocks = []
+
+    def fetch_blocks(upto):
+        for k in range(len(blocks), 0 if resident else min(upto, BLOCKS)):
+            part = pl.ds(k * size, size)
+            blocks.append(fetch(inverse.at[:, part], inverse_v.at[:, part], block_sems.at[k]))
+
+    leak_copy.wait()
     for t in range(tests):
+        for copy in parts[t]:
+            copy.wait()
+        fetch_blocks((t + 1) * BLOCKS // tests)
         centre = own_v[t, 0].astype(jnp.float32)
-        near = above_v[t, 0].astype(jnp.float32) + below_v[t, 0].astype(jnp.float32)
+        near = above_v[t, 0].astype(jnp.float32) * ends[0] + below_v[t, 0].astype(jnp.float32) * ends[1]
         vertical[t * lines : (t + 1) * lines] = (
             centre + leak_v[0] * (near - 2.0 * centre)
         ).astype(jnp.bfloat16)
+    fetch_blocks(BLOCKS)
     sent = []
-    for k in range(0, cells, BLOCK):
-        blocks[k // BLOCK].wait()
+    matrix = inverse if resident else inverse_v
+    for k in range(BLOCKS):
+        if not resident:
+            blocks[k].wait()
         swept = lax.dot_general(
-            vertical[...], inverse_v[0, k : k + BLOCK], NT, preferred_element_type=jnp.float32
+            vertical[...],
+            matrix[0, k * size : (k + 1) * size],
+            NT,
+            preferred_element_type=jnp.float32,
         ).astype(jnp.bfloat16)
-        staged[k : k + BLOCK] = swept.T
+        staged[k * size : (k + 1) * size] = swept.T
         sent.append(
-            fetch(staged.at[pl.ds(k, BLOCK)], out.at[pl.ds(k, BLOCK)], out_sems.at[k // BLOCK])
+            fetch(staged.at[pl.ds(k * size, size)], out.at[pl.ds(k * size, size)], out_sems.at[k])
         )
     for copy in sent:
         copy.wait()
 
 
-def x_sweep(own, first, above, below, leak, inverse, after):
+def x_sweep(own, first, above, below, leak, inverse, ends, after, resident):
     tests, _, lines, width = above.shape
     cells = inverse.shape[1]
     part = pltpu.VMEM(above.shape, above.dtype)
     return pl.pallas_call(
-        functools.partial(x_kernel, first),
-        in_specs=[ANY] * 6,
+        functools.partial(x_kernel, first, len(after), resident),
+        in_specs=[SMEM] + [ANY] * 4 + [VMEM if resident else ANY] + [ANY] * len(after),
         out_specs=ANY,
         out_shape=jax.ShapeDtypeStruct((cells, tests * lines), jnp.bfloat16),
         scratch_shapes=[
@@ -146,17 +182,17 @@
             part,
             part,
             pltpu.VMEM(leak.shape, leak.dtype),
-            pltpu.VMEM(inverse.shape, inverse.dtype),
+            pltpu.VMEM((1, 8, 128) if resident else inverse.shape, inverse.dtype),
             pltpu.VMEM((tests * lines, width), jnp.bfloat16),
             pltpu.VMEM((cells, tests * lines), jnp.bfloat16),
-            pltpu.SemaphoreType.DMA((4,)),
-            pltpu.SemaphoreType.DMA((cells // BLOCK,)),
-            pltpu.SemaphoreType.DMA((cells // BLOCK,)),
+            pltpu.SemaphoreType.DMA((3 * tests + 1,)),
+            pltpu.SemaphoreType.DMA((BLOCKS,)),
+            pltpu.SemaphoreType.DMA((BLOCKS,)),
         ],
-        compiler_params=params(LIMIT),
+        compiler_params=params(RESIDENT_LIMIT if resident else X_LIMIT),
         cost_estimate=cost(2 * cells * tests * lines * width, 20 * MIB),
         name="x_sweep",
-    )(own, above, below, leak, inverse, after)
+    )(ends, own, above, below, leak, inverse, *after)
 
 
 def y_kernel(first, earlier, swept, inverse, hot, weights, *rest):
@@ -182,8 +218,10 @@
 
     group = weights_v.shape[1] // 2 // sources
     place = 0
-    for before in befores:
-        partial[:, place : place + before.shape[1]] = before[...]
+    for i, before in enumerate(befores):
+        inputs.append(
+            fetch(before, partial.at[:, pl.ds(place, before.shape[1])], sems.at[3 + i])
+        )
         place += before.shape[1]
 
     inputs[0].wait()
@@ -253,7 +291,7 @@
             .reshape(partial.shape[0], group, SEG)
             .astype(jnp.bfloat16)
         )
-    for copy in sent:
+    for copy in inputs[3:] + sent:
         copy.wait()
 
 
@@ -266,7 +304,7 @@
     group = weights.shape[1] // 2 // sources
     height = pairs * group + sum(before.shape[1] for before in befores)
     operands = [swept, inverse, hot, weights, *befores]
-    in_specs = [ANY] * 4 + [VMEM] * len(befores)
+    in_specs = [ANY] * len(operands)
     aliases = {}
     if adjoint is not None:
         aliases = {len(operands): 0}
@@ -288,12 +326,12 @@
             pltpu.VMEM((tests * x_local, cells), jnp.bfloat16),
             pltpu.VMEM((tests, 1, x_local, cells), jnp.bfloat16),
             pltpu.VMEM((pairs, rows, 2 * SEG), jnp.float32),
-            pltpu.SemaphoreType.DMA((3,)),
+            pltpu.SemaphoreType.DMA((3 + len(befores),)),
             pltpu.SemaphoreType.DMA((cells // BLOCK,)),
             pltpu.SemaphoreType.DMA((cells // BLOCK,)),
         ],
         input_output_aliases=aliases,
-        compiler_params=params(LIMIT),
+        compiler_params=params(Y_LIMIT),
         cost_estimate=cost(2 * cells * tests * x_local * cells, 20 * MIB),
         name="y_sweep",
     )(*operands)
@@ -305,25 +343,35 @@
     gz_count = lax.axis_size("gz")
     x_local = nx // gx_count
     ny = y_inverse.shape[1]
-    ends = gz_count - 1
-    up = [(i, i + 1) for i in range(ends)]
-    down = [(i + 1, i) for i in range(ends)]
+    up = [(i, (i + 1) % gz_count) for i in range(gz_count)]
+    down = [((i + 1) % gz_count, i) for i in range(gz_count)]
+    layer = lax.axis_index("gz")
+    ends = jnp.stack([layer < gz_count - 1, layer > 0]).astype(jnp.float32)
 
     spans = [(2 * sum(CHUNKS[:c]), 2 * size) for c, size in enumerate(CHUNKS)]
-    arrived = []
-    for first, size in spans:
-        part = split(heads, first, size)
-        arrived.append((lax.ppermute(part, "gz", down), lax.ppermute(part, "gz", up)))
-
+    parts = [split(heads, *spans[0])]
     hot, *weights = prepare(
-        misfit, row_owner, row_count, row_x, row_seg, x_local, ny // SEG, gx_count, gz_count
+        misfit,
+        row_owner,
+        row_count,
+        row_x,
+        row_seg,
+        x_local,
+        ny // SEG,
+        gx_count,
+        gz_count,
+        parts[0],
     )
-
+    later = [split(heads, *span, after=[hot]) for span in spans[2:]]
+    parts += [split(heads, *spans[1], after=later), *later]
+    arrived = [(lax.ppermute(p, "gz", down), lax.ppermute(p, "gz", up)) for p in parts]
     adjoint = None
-    order = [hot, hot]
+    order = [[hot], [], []]
     partials = []
     for c, (first, size) in enumerate(spans):
-        swept = x_sweep(heads, first, *arrived[c], leak, x_inverse, order[c])
+        swept = x_sweep(
+            heads, first, *arrived[c], leak, x_inverse, ends, order[c], False
+        )
         swept = swept.reshape(gx_count, x_local, size * y_local)
         swept = lax.all_to_all(swept, "gx", split_axis=0, concat_axis=0, tiled=True)
         befores = partials if c == len(spans) - 1 else []
@@ -331,7 +379,7 @@
             swept, y_inverse, hot, weights[c], adjoint, befores, first, tests
         )
         partials.append(partial)
-        order.append(partial)
+        order.append([partial])
 
     sent = partials[-1].reshape(gx_count, tests, gz_count, SEG)
     sent = jnp.transpose(sent, (0, 2, 1, 3)).reshape(gx_count * gz_count, tests, SEG)

time: 236 us -> 158 us (0.67)
  Pallas kernels: 128 us -> 62 us
  starting transfers between devices: 58.8 us -> 38.1 us
  waiting for transfers between devices: 20.5 us -> 29.3 us
    pallas_call x9, Pallas kernels: 105 us -> 38.2 us  [the longest x4 30.4 us: x_sweep(): pl.pallas_call(functools.partial(x_kernel, first, len(after), resident),...]
    ppermute x8, starting transfers between devices: 26.8 us -> 12.1 us  [the longest x4 7.12 us: body(): lax.ppermute(p, 'gz', down)]
    all_to_all x4, waiting for transfers between devices: 13.9 us -> 20 us  [body(): swept = lax.all_to_all(swept, 'gx', split_axis=0, concat_axis=0, tiled=True)]
    all_to_all x4, starting transfers between devices: 32 us -> 26 us  [body(): swept = lax.all_to_all(swept, 'gx', split_axis=0, concat_axis=0, tiled=True)]
    ppermute x8, waiting for transfers between devices: 6.57 us -> 9.31 us  [the longest x4 9.22 us: body(): lax.ppermute(p, 'gz', up)]
    unnamed x20 -> x26, local copies, waits for them, and re-layouts: 4.89 us -> 5.85 us
  transfers between devices with their start and end apart: 12 -> 12, of which waited for: 4 -> 8; matrix products, arithmetic and copies ran while one was open for 0% -> 0% of each run, Pallas kernels for 52% -> 35%
where the time goes in v2:
time: 158 us; the launch traced here: 157 us
  Pallas kernels  62 us (39%)
  starting transfers between devices  38.1 us (24%)
  waiting for transfers between devices  29.3 us (19%)
  blocking collectives  19 us (12%)
  local copies, waits for them, and re-layouts  6.08 us (4%)
  between operations  1.6 us (1%)
    pallas_call x4, Pallas kernels, x_sweep(): pl.pallas_call(functools.partial(x_kernel, first, len(after), resident),...  30.4 us
    all_to_all x4, starting transfers between devices, body(): swept = lax.all_to_all(swept, 'gx', split_axis=0, concat_axis=0, tiled=True)  26 us
    pallas_call x4, Pallas kernels, y_sweep(): pl.pallas_call(functools.partial(y_kernel, first, len(befores)), in_specs...  23.8 us
    all_to_all x4, waiting for transfers between devices, body(): swept = lax.all_to_all(swept, 'gx', split_axis=0, concat_axis=0, tiled=True)  20 us
    all_to_all x1, blocking collectives, body(): lax.all_to_all(sent, ('gx', 'gz'), split_axis=0, concat_axis=0, tiled=True)  19 us
    ppermute x4, waiting for transfers between devices, body(): lax.ppermute(p, 'gz', up)  9.22 us
    ppermute x4, starting transfers between devices, body(): lax.ppermute(p, 'gz', down)  7.12 us
    pallas_call x4, Pallas kernels, split(): pl.pallas_call(functools.partial(split_kernel, first), in_specs=[ANY] * (...  6.29 us
  transfers between devices with their start and end apart: 12, of which 8 were waited for; matrix products, arithmetic and copies ran while one was open for 0% of the time, Pallas kernels for 35%

profile of v2, /device:TPU:1, one launch (start us, length us, event | category | flops | bytes accessed | tf_op | source)
XLA Modules:
  0.0 156.9 jit_solution(15809772691550962032)
XLA Ops:
  0.7 1.3 split.4.after
  2.0 2.2 %collective-permute-start.3 = (bf16[4,1,64,2048]{3,2,1,0:T(8,128)(2,1)S(1)}, bf16[4,1,64,2048]{3,2,1,0:T(8,128)(2,1)}, u32[]{:S(2)}, u32[]{:S(2)}) collective-permute-start(bf16[4,1,64,2048]{3,2,1,0:T(8,128)(2,1)S(1)} %split.4.after), channel_id=1, source_target_pairs={{0,1},{1,2},{2,3},{3,0},{4,5},{5,6},{6,7},{7,4},{8,9},{9,10},{10,1... | collective-permute-start | bytes 3145736 | tf_op jit(solution)/shard_map/ppermute | solution.py:367
  4.2 1.5 collective-permute-start.2
  6.4 0.1 copy.14.cells
  6.6 1.5 prepare.1
  8.1 1.0 copy-done.5
  9.0 1.0 copy-done.6
  10.0 1.0 copy-done.7
  11.0 1.0 copy-done.8
  12.0 1.3 split.6.rest_0_
  13.3 1.0 copy-done.3
  14.3 1.3 split.5.rest_1_
  15.6 0.0 copy-start.1
  15.6 1.0 copy-done.1
  16.6 2.3 %split.7 = bf16[4,1,64,2048]{3,2,1,0:T(8,128)(2,1)} custom-call(bf16[16,1,64,2048]{3,2,1,0:T(8,128)(2,1)} %own.7, bf16[4,1,64,2048]{3,2,1,0:T(8,128)(2,1)} %copy-done.3, bf16[4,1,64,2048]{3,2,1,0:T(8,128)(2,1)} %copy-done.1), custom_call_target="tpu_custom_call" | custom-call | bytes 2097152 | tf_op jit(solution)/shard_map/split/pallas_call | solution.py:46
  18.9 0.1 collective-permute-start.5
  19.0 2.7 %collective-permute-start.4 = (bf16[4,1,64,2048]{3,2,1,0:T(8,128)(2,1)}, bf16[4,1,64,2048]{3,2,1,0:T(8,128)(2,1)}, u32[]{:S(2)}, u32[]{:S(2)}) collective-permute-start(bf16[4,1,64,2048]{3,2,1,0:T(8,128)(2,1)} %split.7), channel_id=1, source_target_pairs={{1,0},{2,1},{3,2},{0,3},{5,4},{6,5},{7,6},{4,7},{9,8},{10,9},{11,1... | collective-permute-start | bytes 3145736 | tf_op jit(solution)/shard_map/ppermute | solution.py:367
  21.7 0.1 add_convert_fusion.ends
  21.7 6.8 %collective-permute-done.3.below = bf16[4,1,64,2048]{3,2,1,0:T(8,128)(2,1)} collective-permute-done((bf16[4,1,64,2048]{3,2,1,0:T(8,128)(2,1)S(1)}, bf16[4,1,64,2048]{3,2,1,0:T(8,128)(2,1)}, u32[]{:S(2)}, u32[]{:S(2)}) %collective-permute-start.3) | collective-permute-done | bytes 1048608 | tf_op jit(solution)/shard_map/ppermute | solution.py:367
  28.5 0.0 collective-permute-done.2.above
  28.5 7.6 %x_sweep.4 = bf16[2048,256]{1,0:T(8,128)(2,1)} custom-call(f32[2]{0:T(128)S(1)} %add_convert_fusion.ends, bf16[16,1,64,2048]{3,2,1,0:T(8,128)(2,1)} %own.7, bf16[4,1,64,2048]{3,2,1,0:T(8,128)(2,1)} %collective-permute-done.2.above, bf16[4,1,64,2048]{3,2,1,0:T(8,128)(2,1)} %collective-permute-done.3.below, f32[1,64,2048]{2,1,0:T(8,128)S(1)} %copy-done, ...), custom_call_target="tpu_custom_call" | custom-call | flops 2147483648 | bytes 20971520 | tf_op jit(solution)/shard_map/x_sweep/pallas_call | solution.py:175
  36.1 10.9 %all-to-all-start = ((bf16[32,64,256]{2,1,0:T(8,128)(2,1)}), bf16[32,64,256]{2,1,0:T(8,128)(2,1)}, u32[]{:S(2)}, u32[]{:S(2)}) async-start(bf16[32,64,256]{2,1,0:T(8,128)(2,1)} %bitcast.16), calls=%async_computation | async-start | bytes 2097152 | tf_op jit(solution)/shard_map/all_to_all | solution.py:376
  47.0 0.0 copy-start.2
  47.0 1.4 collective-permute-start.7
  48.4 1.5 collective-permute-start.6
  49.9 1.0 collective-permute-done.5.below
  51.0 7.6 %x_sweep.6 = bf16[2048,256]{1,0:T(8,128)(2,1)} custom-call(f32[2]{0:T(128)S(1)} %add_convert_fusion.ends, bf16[16,1,64,2048]{3,2,1,0:T(8,128)(2,1)} %own.7, bf16[4,1,64,2048]{3,2,1,0:T(8,128)(2,1)} %collective-permute-done.4.above, bf16[4,1,64,2048]{3,2,1,0:T(8,128)(2,1)} %collective-permute-done.5.below, f32[1,64,2048]{2,1,0:T(8,128)S(1)} %copy-done, ...), custom_call_target="tpu_custom_call" | custom-call | flops 2147483648 | bytes 20971520 | tf_op jit(solution)/shard_map/x_sweep/pallas_call | solution.py:175
  58.6 5.6 %all-to-all-done.swept = bf16[32,64,256]{2,1,0:T(8,128)(2,1)} async-done(((bf16[32,64,256]{2,1,0:T(8,128)(2,1)}), bf16[32,64,256]{2,1,0:T(8,128)(2,1)}, u32[]{:S(2)}, u32[]{:S(2)}) %all-to-all-start) | async-done | bytes 1048608 | tf_op jit(solution)/shard_map/all_to_all | solution.py:376
  64.2 5.2 %all-to-all-start.2 = ((bf16[32,64,256]{2,1,0:T(8,128)(2,1)}), bf16[32,64,256]{2,1,0:T(8,128)(2,1)}, u32[]{:S(2)}, u32[]{:S(2)}) async-start(bf16[32,64,256]{2,1,0:T(8,128)(2,1)} %bitcast.7), calls=%async_computation.2 | async-start | bytes 2097152 | tf_op jit(solution)/shard_map/all_to_all | solution.py:376
  69.5 1.4 collective-permute-start.1
  70.8 1.4 collective-permute-start
  72.2 1.4 collective-permute-done.7.below
  73.6 0.1 collective-permute-done.6.above
  73.7 7.6 %x_sweep.7 = bf16[2048,256]{1,0:T(8,128)(2,1)} custom-call(f32[2]{0:T(128)S(1)} %add_convert_fusion.ends, bf16[16,1,64,2048]{3,2,1,0:T(8,128)(2,1)} %own.7, bf16[4,1,64,2048]{3,2,1,0:T(8,128)(2,1)} %collective-permute-done.6.above, bf16[4,1,64,2048]{3,2,1,0:T(8,128)(2,1)} %collective-permute-done.7.below, f32[1,64,2048]{2,1,0:T(8,128)S(1)} %copy-done, ...), custom_call_target="tpu_custom_call" | custom-call | flops 2147483648 | bytes 20971520 | tf_op jit(solution)/shard_map/x_sweep/pallas_call | solution.py:175
  81.3 5.4 %all-to-all-done.2.swept = bf16[32,64,256]{2,1,0:T(8,128)(2,1)} async-done(((bf16[32,64,256]{2,1,0:T(8,128)(2,1)}), bf16[32,64,256]{2,1,0:T(8,128)(2,1)}, u32[]{:S(2)}, u32[]{:S(2)}) %all-to-all-start.2) | async-done | bytes 1048608 | tf_op jit(solution)/shard_map/all_to_all | solution.py:376
  86.7 5.2 %all-to-all-start.3 = ((bf16[32,64,256]{2,1,0:T(8,128)(2,1)}), bf16[32,64,256]{2,1,0:T(8,128)(2,1)S(1)}, u32[]{:S(2)}, u32[]{:S(2)}) async-start(bf16[32,64,256]{2,1,0:T(8,128)(2,1)} %bitcast.8), calls=%async_computation.3 | async-start | bytes 2097152 | tf_op jit(solution)/shard_map/all_to_all | solution.py:376
  91.9 6.0 %y_sweep.4 = (bf16[16,1,64,2048]{3,2,1,0:T(8,128)(2,1)}, bf16[32,16,128]{2,1,0:T(8,128)(2,1)S(1)}) custom-call(bf16[32,64,256]{2,1,0:T(8,128)(2,1)} %all-to-all-done.swept, bf16[1,2048,2048]{2,1,0:T(8,128)(2,1)} %inverse.15, bf16[256,1024]{1,0:T(8,128)(2,1)S(1)} %get-tuple-element.15.rest_0_.hot, bf16[2,512,512]{2,1,0:T(8,128)(2,1)} %copy-done.5), custom_call_target="tpu_custom_call" | custom-call | flops 2147483648 | bytes 20971520 | tf_op jit(solution)/shard_map/y_sweep/pallas_call | solution.py:313
  97.9 0.0 collective-permute-done.1.below
  97.9 7.6 %x_sweep.5 = bf16[2048,256]{1,0:T(8,128)(2,1)} custom-call(f32[2]{0:T(128)S(1)} %add_convert_fusion.ends, bf16[16,1,64,2048]{3,2,1,0:T(8,128)(2,1)} %own.7, bf16[4,1,64,2048]{3,2,1,0:T(8,128)(2,1)} %collective-permute-done.above, bf16[4,1,64,2048]{3,2,1,0:T(8,128)(2,1)} %collective-permute-done.1.below, f32[1,64,2048]{2,1,0:T(8,128)S(1)} %copy-done, ...), custom_call_target="tpu_custom_call" | custom-call | flops 2147483648 | bytes 20971520 | tf_op jit(solution)/shard_map/x_sweep/pallas_call | solution.py:175
  105.5 3.5 %all-to-all-done.3.swept = bf16[32,64,256]{2,1,0:T(8,128)(2,1)S(1)} async-done(((bf16[32,64,256]{2,1,0:T(8,128)(2,1)}), bf16[32,64,256]{2,1,0:T(8,128)(2,1)S(1)}, u32[]{:S(2)}, u32[]{:S(2)}) %all-to-all-start.3) | async-done | bytes 1048608 | tf_op jit(solution)/shard_map/all_to_all | solution.py:376
  109.0 4.7 %all-to-all-start.1 = ((bf16[32,64,256]{2,1,0:T(8,128)(2,1)}), bf16[32,64,256]{2,1,0:T(8,128)(2,1)}, u32[]{:S(2)}, u32[]{:S(2)}) async-start(bf16[32,64,256]{2,1,0:T(8,128)(2,1)} %bitcast.6), calls=%async_computation.1 | async-start | bytes 2097152 | tf_op jit(solution)/shard_map/all_to_all | solution.py:376
  113.8 6.0 %y_sweep.5 = (bf16[16,1,64,2048]{3,2,1,0:T(8,128)(2,1)}, bf16[32,16,128]{2,1,0:T(8,128)(2,1)S(1)}) custom-call(bf16[32,64,256]{2,1,0:T(8,128)(2,1)} %all-to-all-done.2.swept, bf16[1,2048,2048]{2,1,0:T(8,128)(2,1)} %inverse.15, bf16[256,1024]{1,0:T(8,128)(2,1)S(1)} %get-tuple-element.15.rest_0_.hot, ...), custom_call_target="tpu_custom_call", output_to_operand_aliasing={{0}: (4, {})} | custom-call | flops 2147483648 | bytes 20971520 | tf_op jit(solution)/shard_map/y_sweep/pallas_call | solution.py:313
  119.8 5.8 %y_sweep.6 = (bf16[16,1,64,2048]{3,2,1,0:T(8,128)(2,1)}, bf16[32,16,128]{2,1,0:T(8,128)(2,1)S(1)}) custom-call(bf16[32,64,256]{2,1,0:T(8,128)(2,1)S(1)} %all-to-all-done.3.swept, bf16[1,2048,2048]{2,1,0:T(8,128)(2,1)} %inverse.15, bf16[256,1024]{1,0:T(8,128)(2,1)S(1)} %get-tuple-element.15.rest_0_.hot, ...), custom_call_target="tpu_custom_call", output_to_operand_aliasing={{0}: (4, {})} | custom-call | flops 2147483648 | bytes 20971520 | tf_op jit(solution)/shard_map/y_sweep/pallas_call | solution.py:313
  125.6 5.5 %all-to-all-done.1.swept = bf16[32,64,256]{2,1,0:T(8,128)(2,1)} async-done(((bf16[32,64,256]{2,1,0:T(8,128)(2,1)}), bf16[32,64,256]{2,1,0:T(8,128)(2,1)}, u32[]{:S(2)}, u32[]{:S(2)}) %all-to-all-start.1) | async-done | bytes 1048608 | tf_op jit(solution)/shard_map/all_to_all | solution.py:376
  131.0 6.0 %y_sweep.7 = (bf16[16,1,64,2048]{3,2,1,0:T(8,128)(2,1)}, bf16[32,64,128]{2,1,0:T(8,128)(2,1)S(1)}) custom-call(bf16[32,64,256]{2,1,0:T(8,128)(2,1)} %all-to-all-done.1.swept, bf16[1,2048,2048]{2,1,0:T(8,128)(2,1)} %inverse.15, bf16[256,1024]{1,0:T(8,128)(2,1)S(1)} %get-tuple-element.15.rest_0_.hot, ...), custom_call_target="tpu_custom_call", output_to_operand_aliasing={{0}: (7, {})} | custom-call | flops 2147483648 | bytes 20971520 | tf_op jit(solution)/shard_map/y_sweep/pallas_call | solution.py:313
  137.0 0.1 copy.15
  137.1 19.0 %all_to_all.25 = bf16[128,16,128]{2,1,0:T(8,128)(2,1)S(1)} all-to-all(bf16[128,16,128]{2,1,0:T(8,128)(2,1)S(1)} %bitcast.17), channel_id=1, replica_groups=mesh['gx'=32,'gz'=4] {'gx','gz'}, dimensions={0} | all-to-all | bytes 1048576 | tf_op jit(solution)/shard_map/all_to_all | solution.py:386
  156.1 0.7 convert_reduce_fusion
  (22 shorter events, 0.1 us)
Async XLA Ops:
  0.6 5.8 %copy-start.10 = (f32[256,16]{0,1:T(8,128)S(1)}, f32[256,16]{0,1:T(8,128)}, u32[]{:S(2)}) copy-start(f32[256,16]{0,1:T(8,128)} %param.13) | copy-start | bytes 49156
  0.6 5.8 %copy-start.12 = (s32[256]{0:T(256)S(1)}, s32[256]{0:T(256)}, u32[]{:S(2)}) copy-start(s32[256]{0:T(256)} %param.17) | copy-start | bytes 3076
  0.7 5.8 %copy-start.11 = (s32[256]{0:T(256)S(1)}, s32[256]{0:T(256)}, u32[]{:S(2)}) copy-start(s32[256]{0:T(256)} %param.16) | copy-start | bytes 3076
  0.7 5.9 %copy-start.9 = (s32[256,1]{0,1:T(1,128)S(1)}, s32[256,1]{0,1:T(1,128)}, u32[]{:S(2)}) copy-start(s32[256,1]{0,1:T(1,128)} %param.14) | copy-start | bytes 3076
  2.0 26.5 %collective-permute-start.3 = (bf16[4,1,64,2048]{3,2,1,0:T(8,128)(2,1)S(1)}, bf16[4,1,64,2048]{3,2,1,0:T(8,128)(2,1)}, u32[]{:S(2)}, u32[]{:S(2)}) collective-permute-start(bf16[4,1,64,2048]{3,2,1,0:T(8,128)(2,1)S(1)} %split.4.after), channel_id=1, source_target_pairs={{0,1},{1,2},{2,3},{3,0},{4,5},{5,6},{6,7},{7,4},{8,9},{9,10},{10,1... | collective-permute-start | bytes 3145736 | tf_op jit(solution)/shard_map/ppermute | solution.py:367
  4.2 24.3 %collective-permute-start.2 = (bf16[4,1,64,2048]{3,2,1,0:T(8,128)(2,1)S(1)}, bf16[4,1,64,2048]{3,2,1,0:T(8,128)(2,1)}, u32[]{:S(2)}, u32[]{:S(2)}) collective-permute-start(bf16[4,1,64,2048]{3,2,1,0:T(8,128)(2,1)S(1)} %split.4.after), channel_id=1, source_target_pairs={{1,0},{2,1},{3,2},{0,3},{5,4},{6,5},{7,6},{4,7},{9,8},{10,9},{11,1... | collective-permute-start | bytes 3145736 | tf_op jit(solution)/shard_map/ppermute | solution.py:367
  8.1 1.0 copy-start.5
  9.0 1.0 copy-start.6
  10.0 1.0 copy-start.7
  11.0 1.0 copy-start.8
  13.3 1.0 copy-start.3
  15.6 1.0 copy-start.1
  16.6 11.9 %copy-start = (f32[1,64,2048]{2,1,0:T(8,128)S(1)}, f32[1,64,2048]{2,1,0:T(8,128)}, u32[]{:S(2)}) copy-start(f32[1,64,2048]{2,1,0:T(8,128)} %leak.7) | copy-start | bytes 1572868
  18.9 32.1 %collective-permute-start.5 = (bf16[4,1,64,2048]{3,2,1,0:T(8,128)(2,1)}, bf16[4,1,64,2048]{3,2,1,0:T(8,128)(2,1)}, u32[]{:S(2)}, u32[]{:S(2)}) collective-permute-start(bf16[4,1,64,2048]{3,2,1,0:T(8,128)(2,1)} %split.7), channel_id=1, source_target_pairs={{0,1},{1,2},{2,3},{3,0},{4,5},{5,6},{6,7},{7,4},{8,9},{9,10},{10,1... | collective-permute-start | bytes 3145736 | tf_op jit(solution)/shard_map/ppermute | solution.py:367
  19.0 32.0 %collective-permute-start.4 = (bf16[4,1,64,2048]{3,2,1,0:T(8,128)(2,1)}, bf16[4,1,64,2048]{3,2,1,0:T(8,128)(2,1)}, u32[]{:S(2)}, u32[]{:S(2)}) collective-permute-start(bf16[4,1,64,2048]{3,2,1,0:T(8,128)(2,1)} %split.7), channel_id=1, source_target_pairs={{1,0},{2,1},{3,2},{0,3},{5,4},{6,5},{7,6},{4,7},{9,8},{10,9},{11,1... | collective-permute-start | bytes 3145736 | tf_op jit(solution)/shard_map/ppermute | solution.py:367
  21.7 25.2 %copy-start.4 = (bf16[4,1,64,2048]{3,2,1,0:T(8,128)(2,1)S(1)}, bf16[4,1,64,2048]{3,2,1,0:T(8,128)(2,1)}, u32[]{:S(2)}) copy-start(bf16[4,1,64,2048]{3,2,1,0:T(8,128)(2,1)} %copy-done.3) | copy-start | bytes 3145732
  36.1 28.1 %all-to-all-start = ((bf16[32,64,256]{2,1,0:T(8,128)(2,1)}), bf16[32,64,256]{2,1,0:T(8,128)(2,1)}, u32[]{:S(2)}, u32[]{:S(2)}) async-start(bf16[32,64,256]{2,1,0:T(8,128)(2,1)} %bitcast.16), calls=%async_computation | async-start | bytes 2097152 | tf_op jit(solution)/shard_map/all_to_all | solution.py:376
  47.0 22.5 %copy-start.2 = (bf16[4,1,64,2048]{3,2,1,0:T(8,128)(2,1)S(1)}, bf16[4,1,64,2048]{3,2,1,0:T(8,128)(2,1)}, u32[]{:S(2)}) copy-start(bf16[4,1,64,2048]{3,2,1,0:T(8,128)(2,1)} %copy-done.1) | copy-start | bytes 3145732
  47.0 26.6 %collective-permute-start.7 = (bf16[4,1,64,2048]{3,2,1,0:T(8,128)(2,1)S(1)}, bf16[4,1,64,2048]{3,2,1,0:T(8,128)(2,1)}, u32[]{:S(2)}, u32[]{:S(2)}) collective-permute-start(bf16[4,1,64,2048]{3,2,1,0:T(8,128)(2,1)S(1)} %copy-done.4), channel_id=1, source_target_pairs={{0,1},{1,2},{2,3},{3,0},{4,5},{5,6},{6,7},{7,4},{8,9},{9,10},{10,1... | collective-permute-start | bytes 3145736 | tf_op jit(solution)/shard_map/ppermute | solution.py:367
  48.4 25.3 %collective-permute-start.6 = (bf16[4,1,64,2048]{3,2,1,0:T(8,128)(2,1)S(1)}, bf16[4,1,64,2048]{3,2,1,0:T(8,128)(2,1)}, u32[]{:S(2)}, u32[]{:S(2)}) collective-permute-start(bf16[4,1,64,2048]{3,2,1,0:T(8,128)(2,1)S(1)} %copy-done.4), channel_id=1, source_target_pairs={{1,0},{2,1},{3,2},{0,3},{5,4},{6,5},{7,6},{4,7},{9,8},{10,9},{11,1... | collective-permute-start | bytes 3145736 | tf_op jit(solution)/shard_map/ppermute | solution.py:367
  64.2 22.5 %all-to-all-start.2 = ((bf16[32,64,256]{2,1,0:T(8,128)(2,1)}), bf16[32,64,256]{2,1,0:T(8,128)(2,1)}, u32[]{:S(2)}, u32[]{:S(2)}) async-start(bf16[32,64,256]{2,1,0:T(8,128)(2,1)} %bitcast.7), calls=%async_computation.2 | async-start | bytes 2097152 | tf_op jit(solution)/shard_map/all_to_all | solution.py:376
  69.5 28.4 %collective-permute-start.1 = (bf16[4,1,64,2048]{3,2,1,0:T(8,128)(2,1)S(1)}, bf16[4,1,64,2048]{3,2,1,0:T(8,128)(2,1)}, u32[]{:S(2)}, u32[]{:S(2)}) collective-permute-start(bf16[4,1,64,2048]{3,2,1,0:T(8,128)(2,1)S(1)} %copy-done.2), channel_id=1, source_target_pairs={{0,1},{1,2},{2,3},{3,0},{4,5},{5,6},{6,7},{7,4},{8,9},{9,10},{10,1... | collective-permute-start | bytes 3145736 | tf_op jit(solution)/shard_map/ppermute | solution.py:367
  70.8 27.1 %collective-permute-start = (bf16[4,1,64,2048]{3,2,1,0:T(8,128)(2,1)S(1)}, bf16[4,1,64,2048]{3,2,1,0:T(8,128)(2,1)}, u32[]{:S(2)}, u32[]{:S(2)}) collective-permute-start(bf16[4,1,64,2048]{3,2,1,0:T(8,128)(2,1)S(1)} %copy-done.2), channel_id=1, source_target_pairs={{1,0},{2,1},{3,2},{0,3},{5,4},{6,5},{7,6},{4,7},{9,8},{10,9},{11,1... | collective-permute-start | bytes 3145736 | tf_op jit(solution)/shard_map/ppermute | solution.py:367
  86.7 22.3 %all-to-all-start.3 = ((bf16[32,64,256]{2,1,0:T(8,128)(2,1)}), bf16[32,64,256]{2,1,0:T(8,128)(2,1)S(1)}, u32[]{:S(2)}, u32[]{:S(2)}) async-start(bf16[32,64,256]{2,1,0:T(8,128)(2,1)} %bitcast.8), calls=%async_computation.3 | async-start | bytes 2097152 | tf_op jit(solution)/shard_map/all_to_all | solution.py:376
  109.0 22.0 %all-to-all-start.1 = ((bf16[32,64,256]{2,1,0:T(8,128)(2,1)}), bf16[32,64,256]{2,1,0:T(8,128)(2,1)}, u32[]{:S(2)}, u32[]{:S(2)}) async-start(bf16[32,64,256]{2,1,0:T(8,128)(2,1)} %bitcast.6), calls=%async_computation.1 | async-start | bytes 2097152 | tf_op jit(solution)/shard_map/all_to_all | solution.py:376

commit v3 on v2

--- a/solution.py
+++ b/solution.py
@@ -14,10 +14,13 @@
 X_LIMIT = 52
 Y_LIMIT = 52
 LOAD_LIMIT = 50
-RESIDENT_LIMIT = 44
+RESIDENT_LIMIT = 24
+RESIDENT = 1
+LAST_LIMIT = 51
 NT = (((1,), (1,)), ((), ()))
 MIB = 1 << 20
 ANY = pl.BlockSpec(memory_space=pl.ANY)
+HBM = pl.BlockSpec(memory_space=pltpu.HBM)
 VMEM = pl.BlockSpec(memory_space=pltpu.VMEM)
 SMEM = pl.BlockSpec(memory_space=pltpu.SMEM)
 
@@ -42,17 +45,17 @@
     fetch(buffer, out, sems.at[1]).wait()
 
 
-def split(heads, first, size, after=()):
+def split(heads, first, size, after=(), limit=X_LIMIT):
     return pl.pallas_call(
         functools.partial(split_kernel, first),
-        in_specs=[ANY] * (1 + len(after)),
+        in_specs=[HBM] + [ANY] * len(after),
         out_specs=ANY,
         out_shape=jax.ShapeDtypeStruct((size,) + heads.shape[1:], heads.dtype),
         scratch_shapes=[
             pltpu.VMEM((size,) + heads.shape[1:], heads.dtype),
             pltpu.SemaphoreType.DMA((2,)),
         ],
-        compiler_params=params(X_LIMIT),
+        compiler_params=params(limit),
         cost_estimate=cost(0, 2 * MIB),
         name="split",
     )(heads, *after)
@@ -65,7 +68,7 @@
 def load(inverse, after):
     return pl.pallas_call(
         load_kernel,
-        in_specs=[ANY, ANY],
+        in_specs=[HBM, ANY],
         out_specs=VMEM,
         out_shape=pltpu.VMEM(inverse.shape, inverse.dtype),
         scratch_shapes=[pltpu.SemaphoreType.DMA],
@@ -154,13 +157,17 @@
     for k in range(BLOCKS):
         if not resident:
             blocks[k].wait()
-        swept = lax.dot_general(
-            vertical[...],
-            matrix[0, k * size : (k + 1) * size],
-            NT,
-            preferred_element_type=jnp.float32,
-        ).astype(jnp.bfloat16)
-        staged[k * size : (k + 1) * size] = swept.T
+        part = matrix[0, k * size : (k + 1) * size]
+        if resident:
+            staged[k * size : (k + 1) * size] = lax.dot_general(
+                part, vertical[...], NT, preferred_element_type=jnp.float32
+            ).astype(jnp.bfloat16)
+        else:
+            staged[k * size : (k + 1) * size] = (
+                lax.dot_general(vertical[...], part, NT, preferred_element_type=jnp.float32)
+                .astype(jnp.bfloat16)
+                .T
+            )
         sent.append(
             fetch(staged.at[pl.ds(k * size, size)], out.at[pl.ds(k * size, size)], out_sems.at[k])
         )
@@ -174,9 +181,9 @@
     part = pltpu.VMEM(above.shape, above.dtype)
     return pl.pallas_call(
         functools.partial(x_kernel, first, len(after), resident),
-        in_specs=[SMEM] + [ANY] * 4 + [VMEM if resident else ANY] + [ANY] * len(after),
-        out_specs=ANY,
-        out_shape=jax.ShapeDtypeStruct((cells, tests * lines), jnp.bfloat16),
+        in_specs=[SMEM, HBM, ANY, ANY, HBM, VMEM if resident else HBM] + [ANY] * len(after),
+        out_specs=HBM,
+        out_shape=pltpu.HBM((cells, tests * lines), jnp.bfloat16),
         scratch_shapes=[
             part,
             part,
@@ -295,7 +302,7 @@
         copy.wait()
 
 
-def y_sweep(swept, inverse, hot, weights, adjoint, befores, first, tests_total):
+def y_sweep(swept, inverse, hot, weights, adjoint, befores, first, tests_total, limit):
     sources, x_local, lanes = swept.shape
     pairs = lanes // SEG
     tests = 2 * pairs
@@ -304,7 +311,7 @@
     group = weights.shape[1] // 2 // sources
     height = pairs * group + sum(before.shape[1] for before in befores)
     operands = [swept, inverse, hot, weights, *befores]
-    in_specs = [ANY] * len(operands)
+    in_specs = [ANY] + [HBM] * 3 + [ANY] * len(befores)
     aliases = {}
     if adjoint is not None:
         aliases = {len(operands): 0}
@@ -331,7 +338,7 @@
             pltpu.SemaphoreType.DMA((cells // BLOCK,)),
         ],
         input_output_aliases=aliases,
-        compiler_params=params(Y_LIMIT),
+        compiler_params=params(limit),
         cost_estimate=cost(2 * cells * tests * x_local * cells, 20 * MIB),
         name="y_sweep",
     )(*operands)
@@ -369,14 +376,22 @@
     order = [[hot], [], []]
     partials = []
     for c, (first, size) in enumerate(spans):
-        swept = x_sweep(
-            heads, first, *arrived[c], leak, x_inverse, ends, order[c], False
-        )
-        swept = swept.reshape(gx_count, x_local, size * y_local)
+        resident = c < RESIDENT
+        matrix = load(x_inverse, parts[1] if c == 0 else lines) if resident else x_inverse
+        lines = x_sweep(heads, first, *arrived[c], leak, matrix, ends, order[c], resident)
+        swept = lines.reshape(gx_count, x_local, size * y_local)
         swept = lax.all_to_all(swept, "gx", split_axis=0, concat_axis=0, tiled=True)
         befores = partials if c == len(spans) - 1 else []
         adjoint, partial = y_sweep(
-            swept, y_inverse, hot, weights[c], adjoint, befores, first, tests
+            swept,
+            y_inverse,
+            hot,
+            weights[c],
+            adjoint,
+            befores,
+            first,
+            tests,
+            LAST_LIMIT if befores else Y_LIMIT,
         )
         partials.append(partial)
         order.append([partial])

time: 158 us -> 159 us (level)
  Pallas kernels: 62 us -> 64.6 us
  blocking collectives: 19 us -> 17.1 us
    pallas_call x4 -> x5, Pallas kernels: 6.29 us -> 10.6 us  [the longest x4 7.09 us: split(): pl.pallas_call(functools.partial(split_kernel, first), in_specs=[HBM] + [...]
    ppermute x4, waiting for transfers between devices: 0.09 us -> 3.09 us  [body(): lax.ppermute(p, 'gz', down)]
    ppermute x4, starting transfers between devices: 4.99 us -> 2.91 us  [body(): lax.ppermute(p, 'gz', up)]
    all_to_all x1, blocking collectives: 19 us -> 17.1 us  [body(): lax.all_to_all(sent, ('gx', 'gz'), split_axis=0, concat_axis=0, tiled=True)]
    pallas_call x4, Pallas kernels: 30.4 us -> 28.7 us  [x_sweep(): pl.pallas_call(functools.partial(x_kernel, first, len(after), resident),...]
  transfers between devices with their start and end apart: 12 -> 12, of which waited for: 8 -> 9; matrix products, arithmetic and copies ran while one was open for 0% -> 0% of each run, Pallas kernels for 35% -> 36%
where the time goes in v3:
time: 159 us; the launch traced here: 158 us
  Pallas kernels  64.6 us (41%)
  starting transfers between devices  36.9 us (23%)
  waiting for transfers between devices  30.7 us (19%)
  blocking collectives  17.1 us (11%)
  local copies, waits for them, and re-layouts  6.22 us (4%)
  between operations  1.59 us (1%)
    pallas_call x4, Pallas kernels, x_sweep(): pl.pallas_call(functools.partial(x_kernel, first, len(after), resident),...  28.7 us
    all_to_all x4, starting transfers between devices, body(): swept = lax.all_to_all(swept, 'gx', split_axis=0, concat_axis=0, tiled=True)  27.4 us
    pallas_call x4, Pallas kernels, y_sweep(): pl.pallas_call(functools.partial(y_kernel, first, len(befores)), in_specs...  23.8 us
    all_to_all x4, waiting for transfers between devices, body(): swept = lax.all_to_all(swept, 'gx', split_axis=0, concat_axis=0, tiled=True)  19.4 us
    all_to_all x1, blocking collectives, body(): lax.all_to_all(sent, ('gx', 'gz'), split_axis=0, concat_axis=0, tiled=True)  17.1 us
    ppermute x4, waiting for transfers between devices, body(): lax.ppermute(p, 'gz', up)  8.17 us
    pallas_call x4, Pallas kernels, split(): pl.pallas_call(functools.partial(split_kernel, first), in_specs=[HBM] + [...  7.09 us
    ppermute x4, starting transfers between devices, body(): lax.ppermute(p, 'gz', down)  6.52 us
  transfers between devices with their start and end apart: 12, of which 9 were waited for; matrix products, arithmetic and copies ran while one was open for 0% of the time, Pallas kernels for 36%

profile of v3, /device:TPU:1, one launch (start us, length us, event | category | flops | bytes accessed | tf_op | source)
XLA Modules:
  0.0 157.9 jit_solution(2272569014230769251)
XLA Ops:
  0.7 2.2 %split.4.after = bf16[4,1,64,2048]{3,2,1,0:T(8,128)(2,1)} custom-call(bf16[16,1,64,2048]{3,2,1,0:T(8,128)(2,1)} %own.7), custom_call_target="tpu_custom_call" | custom-call | bytes 2097152 | tf_op jit(solution)/shard_map/split/pallas_call | solution.py:49
  2.9 3.6 %collective-permute-start.2 = (bf16[4,1,64,2048]{3,2,1,0:T(8,128)(2,1)}, bf16[4,1,64,2048]{3,2,1,0:T(8,128)(2,1)}, u32[]{:S(2)}, u32[]{:S(2)}) collective-permute-start(bf16[4,1,64,2048]{3,2,1,0:T(8,128)(2,1)} %split.4.after), channel_id=1, source_target_pairs={{1,0},{2,1},{3,2},{0,3},{5,4},{6,5},{7,6},{4,7},{9,8},{10,9},{11,1... | collective-permute-start | bytes 3145736 | tf_op jit(solution)/shard_map/ppermute | solution.py:374
  6.5 0.0 collective-permute-start.3
  6.6 0.1 copy.14.cells
  7.4 1.5 prepare.1
  8.9 1.0 copy-done.5
  9.8 1.0 copy-done.6
  10.8 1.0 copy-done.7
  11.8 1.0 copy-done.8
  12.8 1.3 split.5.rest_1_
  14.1 1.1 copy-done.2
  15.2 1.3 split.6.rest_0_
  16.5 1.0 copy-done.4
  17.5 2.2 %split.7.after = bf16[4,1,64,2048]{3,2,1,0:T(8,128)(2,1)} custom-call(bf16[16,1,64,2048]{3,2,1,0:T(8,128)(2,1)} %own.7, bf16[4,1,64,2048]{3,2,1,0:T(8,128)(2,1)} %copy-done.4, bf16[4,1,64,2048]{3,2,1,0:T(8,128)(2,1)} %copy-done.2), custom_call_target="tpu_custom_call" | custom-call | bytes 2097152 | tf_op jit(solution)/shard_map/split/pallas_call | solution.py:49
  19.7 2.7 %collective-permute-start.4 = (bf16[4,1,64,2048]{3,2,1,0:T(8,128)(2,1)}, bf16[4,1,64,2048]{3,2,1,0:T(8,128)(2,1)}, u32[]{:S(2)}, u32[]{:S(2)}) collective-permute-start(bf16[4,1,64,2048]{3,2,1,0:T(8,128)(2,1)} %split.7.after), channel_id=1, source_target_pairs={{1,0},{2,1},{3,2},{0,3},{5,4},{6,5},{7,6},{4,7},{9,8},{10,9},{11,1... | collective-permute-start | bytes 3145736 | tf_op jit(solution)/shard_map/ppermute | solution.py:374
  22.5 0.0 collective-permute-start.5
  22.5 0.1 add_convert_fusion.ends
  22.6 3.5 %load.1.inverse = bf16[1,2048,2048]{2,1,0:T(8,128)(2,1)S(1)} custom-call(bf16[1,2048,2048]{2,1,0:T(8,128)(2,1)} %inverse.11, bf16[4,1,64,2048]{3,2,1,0:T(8,128)(2,1)} %split.7.after), custom_call_target="tpu_custom_call" | custom-call | bytes 16777216 | tf_op jit(solution)/shard_map/load/pallas_call | solution.py:69
  26.1 2.6 %collective-permute-done.2.above = bf16[4,1,64,2048]{3,2,1,0:T(8,128)(2,1)} collective-permute-done((bf16[4,1,64,2048]{3,2,1,0:T(8,128)(2,1)}, bf16[4,1,64,2048]{3,2,1,0:T(8,128)(2,1)}, u32[]{:S(2)}, u32[]{:S(2)}) %collective-permute-start.2) | collective-permute-done | bytes 1048608 | tf_op jit(solution)/shard_map/ppermute | solution.py:374
  28.7 3.1 %collective-permute-done.3.below = bf16[4,1,64,2048]{3,2,1,0:T(8,128)(2,1)} collective-permute-done((bf16[4,1,64,2048]{3,2,1,0:T(8,128)(2,1)}, bf16[4,1,64,2048]{3,2,1,0:T(8,128)(2,1)}, u32[]{:S(2)}, u32[]{:S(2)}) %collective-permute-start.3) | collective-permute-done | bytes 1048608 | tf_op jit(solution)/shard_map/ppermute | solution.py:374
  31.8 6.0 %x_sweep.4 = bf16[2048,256]{1,0:T(8,128)(2,1)} custom-call(f32[2]{0:T(128)S(1)} %add_convert_fusion.ends, bf16[16,1,64,2048]{3,2,1,0:T(8,128)(2,1)S(1)} %copy-done, bf16[4,1,64,2048]{3,2,1,0:T(8,128)(2,1)} %collective-permute-done.2.above, bf16[4,1,64,2048]{3,2,1,0:T(8,128)(2,1)} %collective-permute-done.3.below, f32[1,64,2048]{2,1,0:T(8,128)S(1)} %copy-done.1, ...), custom_call_target="tpu_custom_call" | custom-call | flops 2147483648 | bytes 20971520 | tf_op jit(solution)/shard_map/x_sweep/pallas_call | solution.py:182
  37.8 11.3 %all-to-all-start = ((bf16[32,64,256]{2,1,0:T(8,128)(2,1)}), bf16[32,64,256]{2,1,0:T(8,128)(2,1)}, u32[]{:S(2)}, u32[]{:S(2)}) async-start(bf16[32,64,256]{2,1,0:T(8,128)(2,1)} %bitcast.18), calls=%async_computation | async-start | bytes 2097152 | tf_op jit(solution)/shard_map/all_to_all | solution.py:383
  49.1 0.1 collective-permute-start.6
  49.2 1.5 collective-permute-start.7
  50.6 0.5 collective-permute-done.4.above
  51.2 3.1 %collective-permute-done.5.below = bf16[4,1,64,2048]{3,2,1,0:T(8,128)(2,1)} collective-permute-done((bf16[4,1,64,2048]{3,2,1,0:T(8,128)(2,1)}, bf16[4,1,64,2048]{3,2,1,0:T(8,128)(2,1)}, u32[]{:S(2)}, u32[]{:S(2)}) %collective-permute-start.5) | collective-permute-done | bytes 1048608 | tf_op jit(solution)/shard_map/ppermute | solution.py:374
  54.3 7.6 %x_sweep.6 = bf16[2048,256]{1,0:T(8,128)(2,1)} custom-call(f32[2]{0:T(128)S(1)} %add_convert_fusion.ends, bf16[16,1,64,2048]{3,2,1,0:T(8,128)(2,1)} %own.7, bf16[4,1,64,2048]{3,2,1,0:T(8,128)(2,1)} %collective-permute-done.4.above, bf16[4,1,64,2048]{3,2,1,0:T(8,128)(2,1)} %collective-permute-done.5.below, f32[1,64,2048]{2,1,0:T(8,128)S(1)} %copy-done.1, ...), custom_call_target="tpu_custom_call" | custom-call | flops 2147483648 | bytes 20971520 | tf_op jit(solution)/shard_map/x_sweep/pallas_call | solution.py:182
  61.8 4.5 %all-to-all-done.swept = bf16[32,64,256]{2,1,0:T(8,128)(2,1)} async-done(((bf16[32,64,256]{2,1,0:T(8,128)(2,1)}), bf16[32,64,256]{2,1,0:T(8,128)(2,1)}, u32[]{:S(2)}, u32[]{:S(2)}) %all-to-all-start) | async-done | bytes 1048608 | tf_op jit(solution)/shard_map/all_to_all | solution.py:383
  66.3 6.9 %all-to-all-start.2 = ((bf16[32,64,256]{2,1,0:T(8,128)(2,1)}), bf16[32,64,256]{2,1,0:T(8,128)(2,1)}, u32[]{:S(2)}, u32[]{:S(2)}) async-start(bf16[32,64,256]{2,1,0:T(8,128)(2,1)} %bitcast.16), calls=%async_computation.2 | async-start | bytes 2097152 | tf_op jit(solution)/shard_map/all_to_all | solution.py:383
  73.2 0.1 collective-permute-start
  73.3 1.5 collective-permute-start.1
  74.7 0.0 collective-permute-done.6.above
  74.7 2.0 %collective-permute-done.7.below = bf16[4,1,64,2048]{3,2,1,0:T(8,128)(2,1)} collective-permute-done((bf16[4,1,64,2048]{3,2,1,0:T(8,128)(2,1)}, bf16[4,1,64,2048]{3,2,1,0:T(8,128)(2,1)}, u32[]{:S(2)}, u32[]{:S(2)}) %collective-permute-start.7) | collective-permute-done | bytes 1048608 | tf_op jit(solution)/shard_map/ppermute | solution.py:374
  76.7 7.6 %x_sweep.7 = bf16[2048,256]{1,0:T(8,128)(2,1)} custom-call(f32[2]{0:T(128)S(1)} %add_convert_fusion.ends, bf16[16,1,64,2048]{3,2,1,0:T(8,128)(2,1)} %own.7, bf16[4,1,64,2048]{3,2,1,0:T(8,128)(2,1)} %collective-permute-done.6.above, bf16[4,1,64,2048]{3,2,1,0:T(8,128)(2,1)} %collective-permute-done.7.below, f32[1,64,2048]{2,1,0:T(8,128)S(1)} %copy-done.1, ...), custom_call_target="tpu_custom_call" | custom-call | flops 2147483648 | bytes 20971520 | tf_op jit(solution)/shard_map/x_sweep/pallas_call | solution.py:182
  84.3 6.1 %all-to-all-done.2.swept = bf16[32,64,256]{2,1,0:T(8,128)(2,1)} async-done(((bf16[32,64,256]{2,1,0:T(8,128)(2,1)}), bf16[32,64,256]{2,1,0:T(8,128)(2,1)}, u32[]{:S(2)}, u32[]{:S(2)}) %all-to-all-start.2) | async-done | bytes 1048608 | tf_op jit(solution)/shard_map/all_to_all | solution.py:383
  90.4 5.3 %all-to-all-start.3 = ((bf16[32,64,256]{2,1,0:T(8,128)(2,1)}), bf16[32,64,256]{2,1,0:T(8,128)(2,1)}, u32[]{:S(2)}, u32[]{:S(2)}) async-start(bf16[32,64,256]{2,1,0:T(8,128)(2,1)} %bitcast.17), calls=%async_computation.3 | async-start | bytes 2097152 | tf_op jit(solution)/shard_map/all_to_all | solution.py:383
  95.7 6.0 %y_sweep.4 = (bf16[16,1,64,2048]{3,2,1,0:T(8,128)(2,1)}, bf16[32,16,128]{2,1,0:T(8,128)(2,1)S(1)}) custom-call(bf16[32,64,256]{2,1,0:T(8,128)(2,1)} %all-to-all-done.swept, bf16[1,2048,2048]{2,1,0:T(8,128)(2,1)} %inverse.13, bf16[256,1024]{1,0:T(8,128)(2,1)S(1)} %get-tuple-element.15.rest_0_.hot, bf16[2,512,512]{2,1,0:T(8,128)(2,1)} %copy-done.5), custom_call_target="tpu_custom_call" | custom-call | flops 2147483648 | bytes 20971520 | tf_op jit(solution)/shard_map/y_sweep/pallas_call | solution.py:320
  101.7 0.0 collective-permute-done.1.below
  101.7 7.6 %x_sweep.5 = bf16[2048,256]{1,0:T(8,128)(2,1)} custom-call(f32[2]{0:T(128)S(1)} %add_convert_fusion.ends, bf16[16,1,64,2048]{3,2,1,0:T(8,128)(2,1)} %own.7, bf16[4,1,64,2048]{3,2,1,0:T(8,128)(2,1)} %collective-permute-done.above, bf16[4,1,64,2048]{3,2,1,0:T(8,128)(2,1)} %collective-permute-done.1.below, f32[1,64,2048]{2,1,0:T(8,128)S(1)} %copy-done.1, ...), custom_call_target="tpu_custom_call" | custom-call | flops 2147483648 | bytes 20971520 | tf_op jit(solution)/shard_map/x_sweep/pallas_call | solution.py:182
  109.3 3.6 %all-to-all-done.3.swept = bf16[32,64,256]{2,1,0:T(8,128)(2,1)} async-done(((bf16[32,64,256]{2,1,0:T(8,128)(2,1)}), bf16[32,64,256]{2,1,0:T(8,128)(2,1)}, u32[]{:S(2)}, u32[]{:S(2)}) %all-to-all-start.3) | async-done | bytes 1048608 | tf_op jit(solution)/shard_map/all_to_all | solution.py:383
  112.9 4.0 %all-to-all-start.1 = ((bf16[32,64,256]{2,1,0:T(8,128)(2,1)}), bf16[32,64,256]{2,1,0:T(8,128)(2,1)S(1)}, u32[]{:S(2)}, u32[]{:S(2)}) async-start(bf16[32,64,256]{2,1,0:T(8,128)(2,1)} %bitcast.19), calls=%async_computation.1 | async-start | bytes 2097152 | tf_op jit(solution)/shard_map/all_to_all | solution.py:383
  116.9 6.0 %y_sweep.5 = (bf16[16,1,64,2048]{3,2,1,0:T(8,128)(2,1)}, bf16[32,16,128]{2,1,0:T(8,128)(2,1)S(1)}) custom-call(bf16[32,64,256]{2,1,0:T(8,128)(2,1)} %all-to-all-done.2.swept, bf16[1,2048,2048]{2,1,0:T(8,128)(2,1)} %inverse.13, bf16[256,1024]{1,0:T(8,128)(2,1)S(1)} %get-tuple-element.15.rest_0_.hot, ...), custom_call_target="tpu_custom_call", output_to_operand_aliasing={{0}: (4, {})} | custom-call | flops 2147483648 | bytes 20971520 | tf_op jit(solution)/shard_map/y_sweep/pallas_call | solution.py:320
  122.9 6.0 %y_sweep.6 = (bf16[16,1,64,2048]{3,2,1,0:T(8,128)(2,1)}, bf16[32,16,128]{2,1,0:T(8,128)(2,1)S(1)}) custom-call(bf16[32,64,256]{2,1,0:T(8,128)(2,1)} %all-to-all-done.3.swept, bf16[1,2048,2048]{2,1,0:T(8,128)(2,1)} %inverse.13, bf16[256,1024]{1,0:T(8,128)(2,1)S(1)} %get-tuple-element.15.rest_0_.hot, ...), custom_call_target="tpu_custom_call", output_to_operand_aliasing={{0}: (4, {})} | custom-call | flops 2147483648 | bytes 20971520 | tf_op jit(solution)/shard_map/y_sweep/pallas_call | solution.py:320
  128.9 5.3 %all-to-all-done.1.swept = bf16[32,64,256]{2,1,0:T(8,128)(2,1)S(1)} async-done(((bf16[32,64,256]{2,1,0:T(8,128)(2,1)}), bf16[32,64,256]{2,1,0:T(8,128)(2,1)S(1)}, u32[]{:S(2)}, u32[]{:S(2)}) %all-to-all-start.1) | async-done | bytes 1048608 | tf_op jit(solution)/shard_map/all_to_all | solution.py:383
  134.2 5.8 %y_sweep.7 = (bf16[16,1,64,2048]{3,2,1,0:T(8,128)(2,1)}, bf16[32,64,128]{2,1,0:T(8,128)(2,1)S(1)}) custom-call(bf16[32,64,256]{2,1,0:T(8,128)(2,1)S(1)} %all-to-all-done.1.swept, bf16[1,2048,2048]{2,1,0:T(8,128)(2,1)} %inverse.13, bf16[256,1024]{1,0:T(8,128)(2,1)S(1)} %get-tuple-element.15.rest_0_.hot, ...), custom_call_target="tpu_custom_call", output_to_operand_aliasing={{0}: (7, {})} | custom-call | flops 2147483648 | bytes 20971520 | tf_op jit(solution)/shard_map/y_sweep/pallas_call | solution.py:320
  140.0 0.1 copy.15
  140.1 17.1 %all_to_all.25 = bf16[128,16,128]{2,1,0:T(8,128)(2,1)S(1)} all-to-all(bf16[128,16,128]{2,1,0:T(8,128)(2,1)S(1)} %bitcast.20), channel_id=1, replica_groups=mesh['gx'=32,'gz'=4] {'gx','gz'}, dimensions={0} | all-to-all | bytes 1048576 | tf_op jit(solution)/shard_map/all_to_all | solution.py:401
  157.1 0.7 convert_reduce_fusion
  (23 shorter events, 0.1 us)
Async XLA Ops:
  0.6 5.9 %copy-start.11 = (s32[256]{0:T(256)S(1)}, s32[256]{0:T(256)}, u32[]{:S(2)}) copy-start(s32[256]{0:T(256)} %param.16) | copy-start | bytes 3076
  0.6 5.9 %copy-start.12 = (s32[256]{0:T(256)S(1)}, s32[256]{0:T(256)}, u32[]{:S(2)}) copy-start(s32[256]{0:T(256)} %param.17) | copy-start | bytes 3076
  0.7 6.1 %copy-start.10 = (f32[256,16]{0,1:T(8,128)S(1)}, f32[256,16]{0,1:T(8,128)}, u32[]{:S(2)}) copy-start(f32[256,16]{0,1:T(8,128)} %param.13) | copy-start | bytes 49156
  0.7 6.7 %copy-start.9 = (s32[256,1]{0,1:T(1,128)S(1)}, s32[256,1]{0,1:T(1,128)}, u32[]{:S(2)}) copy-start(s32[256,1]{0,1:T(1,128)} %param.14) | copy-start | bytes 3076
  2.9 25.8 %collective-permute-start.2 = (bf16[4,1,64,2048]{3,2,1,0:T(8,128)(2,1)}, bf16[4,1,64,2048]{3,2,1,0:T(8,128)(2,1)}, u32[]{:S(2)}, u32[]{:S(2)}) collective-permute-start(bf16[4,1,64,2048]{3,2,1,0:T(8,128)(2,1)} %split.4.after), channel_id=1, source_target_pairs={{1,0},{2,1},{3,2},{0,3},{5,4},{6,5},{7,6},{4,7},{9,8},{10,9},{11,1... | collective-permute-start | bytes 3145736 | tf_op jit(solution)/shard_map/ppermute | solution.py:374
  6.5 25.2 %collective-permute-start.3 = (bf16[4,1,64,2048]{3,2,1,0:T(8,128)(2,1)}, bf16[4,1,64,2048]{3,2,1,0:T(8,128)(2,1)}, u32[]{:S(2)}, u32[]{:S(2)}) collective-permute-start(bf16[4,1,64,2048]{3,2,1,0:T(8,128)(2,1)} %split.4.after), channel_id=1, source_target_pairs={{0,1},{1,2},{2,3},{3,0},{4,5},{5,6},{6,7},{7,4},{8,9},{9,10},{10,1... | collective-permute-start | bytes 3145736 | tf_op jit(solution)/shard_map/ppermute | solution.py:374
  8.9 1.0 copy-start.5
  9.8 1.0 copy-start.6
  10.8 1.0 copy-start.7
  11.8 1.0 copy-start.8
  14.1 1.1 copy-start.2
  16.5 1.0 copy-start.4
  19.7 31.4 %collective-permute-start.4 = (bf16[4,1,64,2048]{3,2,1,0:T(8,128)(2,1)}, bf16[4,1,64,2048]{3,2,1,0:T(8,128)(2,1)}, u32[]{:S(2)}, u32[]{:S(2)}) collective-permute-start(bf16[4,1,64,2048]{3,2,1,0:T(8,128)(2,1)} %split.7.after), channel_id=1, source_target_pairs={{1,0},{2,1},{3,2},{0,3},{5,4},{6,5},{7,6},{4,7},{9,8},{10,9},{11,1... | collective-permute-start | bytes 3145736 | tf_op jit(solution)/shard_map/ppermute | solution.py:374
  22.5 31.8 %collective-permute-start.5 = (bf16[4,1,64,2048]{3,2,1,0:T(8,128)(2,1)}, bf16[4,1,64,2048]{3,2,1,0:T(8,128)(2,1)}, u32[]{:S(2)}, u32[]{:S(2)}) collective-permute-start(bf16[4,1,64,2048]{3,2,1,0:T(8,128)(2,1)} %split.7.after), channel_id=1, source_target_pairs={{0,1},{1,2},{2,3},{3,0},{4,5},{5,6},{6,7},{7,4},{8,9},{9,10},{10,1... | collective-permute-start | bytes 3145736 | tf_op jit(solution)/shard_map/ppermute | solution.py:374
  22.6 9.2 %copy-start = (bf16[16,1,64,2048]{3,2,1,0:T(8,128)(2,1)S(1)}, bf16[16,1,64,2048]{3,2,1,0:T(8,128)(2,1)}, u32[]{:S(2)}) copy-start(bf16[16,1,64,2048]{3,2,1,0:T(8,128)(2,1)} %own.7) | copy-start | bytes 12582916
  22.6 9.2 %copy-start.1 = (f32[1,64,2048]{2,1,0:T(8,128)S(1)}, f32[1,64,2048]{2,1,0:T(8,128)}, u32[]{:S(2)}) copy-start(f32[1,64,2048]{2,1,0:T(8,128)} %leak.7) | copy-start | bytes 1572868
  37.8 28.6 %all-to-all-start = ((bf16[32,64,256]{2,1,0:T(8,128)(2,1)}), bf16[32,64,256]{2,1,0:T(8,128)(2,1)}, u32[]{:S(2)}, u32[]{:S(2)}) async-start(bf16[32,64,256]{2,1,0:T(8,128)(2,1)} %bitcast.18), calls=%async_computation | async-start | bytes 2097152 | tf_op jit(solution)/shard_map/all_to_all | solution.py:383
  49.1 24.1 %copy-start.3 = (bf16[4,1,64,2048]{3,2,1,0:T(8,128)(2,1)S(1)}, bf16[4,1,64,2048]{3,2,1,0:T(8,128)(2,1)}, u32[]{:S(2)}) copy-start(bf16[4,1,64,2048]{3,2,1,0:T(8,128)(2,1)} %copy-done.2) | copy-start | bytes 3145732
  49.1 25.6 %collective-permute-start.6 = (bf16[4,1,64,2048]{3,2,1,0:T(8,128)(2,1)}, bf16[4,1,64,2048]{3,2,1,0:T(8,128)(2,1)}, u32[]{:S(2)}, u32[]{:S(2)}) collective-permute-start(bf16[4,1,64,2048]{3,2,1,0:T(8,128)(2,1)} %copy-done.4), channel_id=1, source_target_pairs={{1,0},{2,1},{3,2},{0,3},{5,4},{6,5},{7,6},{4,7},{9,8},{10,9},{11,1... | collective-permute-start | bytes 3145736 | tf_op jit(solution)/shard_map/ppermute | solution.py:374
  49.2 27.5 %collective-permute-start.7 = (bf16[4,1,64,2048]{3,2,1,0:T(8,128)(2,1)}, bf16[4,1,64,2048]{3,2,1,0:T(8,128)(2,1)}, u32[]{:S(2)}, u32[]{:S(2)}) collective-permute-start(bf16[4,1,64,2048]{3,2,1,0:T(8,128)(2,1)} %copy-done.4), channel_id=1, source_target_pairs={{0,1},{1,2},{2,3},{3,0},{4,5},{5,6},{6,7},{7,4},{8,9},{9,10},{10,1... | collective-permute-start | bytes 3145736 | tf_op jit(solution)/shard_map/ppermute | solution.py:374
  66.3 24.1 %all-to-all-start.2 = ((bf16[32,64,256]{2,1,0:T(8,128)(2,1)}), bf16[32,64,256]{2,1,0:T(8,128)(2,1)}, u32[]{:S(2)}, u32[]{:S(2)}) async-start(bf16[32,64,256]{2,1,0:T(8,128)(2,1)} %bitcast.16), calls=%async_computation.2 | async-start | bytes 2097152 | tf_op jit(solution)/shard_map/all_to_all | solution.py:383
  73.2 28.5 %collective-permute-start = (bf16[4,1,64,2048]{3,2,1,0:T(8,128)(2,1)S(1)}, bf16[4,1,64,2048]{3,2,1,0:T(8,128)(2,1)}, u32[]{:S(2)}, u32[]{:S(2)}) collective-permute-start(bf16[4,1,64,2048]{3,2,1,0:T(8,128)(2,1)S(1)} %copy-done.3), channel_id=1, source_target_pairs={{1,0},{2,1},{3,2},{0,3},{5,4},{6,5},{7,6},{4,7},{9,8},{10,9},{11,1... | collective-permute-start | bytes 3145736 | tf_op jit(solution)/shard_map/ppermute | solution.py:374
  73.3 28.4 %collective-permute-start.1 = (bf16[4,1,64,2048]{3,2,1,0:T(8,128)(2,1)S(1)}, bf16[4,1,64,2048]{3,2,1,0:T(8,128)(2,1)}, u32[]{:S(2)}, u32[]{:S(2)}) collective-permute-start(bf16[4,1,64,2048]{3,2,1,0:T(8,128)(2,1)S(1)} %copy-done.3), channel_id=1, source_target_pairs={{0,1},{1,2},{2,3},{3,0},{4,5},{5,6},{6,7},{7,4},{8,9},{9,10},{10,1... | collective-permute-start | bytes 3145736 | tf_op jit(solution)/shard_map/ppermute | solution.py:374
  90.4 22.5 %all-to-all-start.3 = ((bf16[32,64,256]{2,1,0:T(8,128)(2,1)}), bf16[32,64,256]{2,1,0:T(8,128)(2,1)}, u32[]{:S(2)}, u32[]{:S(2)}) async-start(bf16[32,64,256]{2,1,0:T(8,128)(2,1)} %bitcast.17), calls=%async_computation.3 | async-start | bytes 2097152 | tf_op jit(solution)/shard_map/all_to_all | solution.py:383
  112.9 21.3 %all-to-all-start.1 = ((bf16[32,64,256]{2,1,0:T(8,128)(2,1)}), bf16[32,64,256]{2,1,0:T(8,128)(2,1)S(1)}, u32[]{:S(2)}, u32[]{:S(2)}) async-start(bf16[32,64,256]{2,1,0:T(8,128)(2,1)} %bitcast.19), calls=%async_computation.1 | async-start | bytes 2097152 | tf_op jit(solution)/shard_map/all_to_all | solution.py:383

commit v4 on v3

--- a/solution.py
+++ b/solution.py
@@ -15,10 +15,11 @@
 Y_LIMIT = 52
 LOAD_LIMIT = 50
 RESIDENT_LIMIT = 24
-RESIDENT = 1
+RESIDENT = 2
 LAST_LIMIT = 51
 NT = (((1,), (1,)), ((), ()))
 MIB = 1 << 20
+SCALE = 1
 ANY = pl.BlockSpec(memory_space=pl.ANY)
 HBM = pl.BlockSpec(memory_space=pltpu.HBM)
 VMEM = pl.BlockSpec(memory_space=pltpu.VMEM)
@@ -30,7 +31,7 @@
 
 
 def cost(flops, nbytes):
-    return pl.CostEstimate(flops=flops, bytes_accessed=nbytes, transcendentals=0)
+    return pl.CostEstimate(flops=flops // SCALE, bytes_accessed=nbytes // SCALE, transcendentals=0)
 
 
 def fetch(source, buffer, sem):
@@ -45,12 +46,12 @@
     fetch(buffer, out, sems.at[1]).wait()
 
 
-def split(heads, first, size, after=(), limit=X_LIMIT):
+def split(heads, first, size, after=(), limit=X_LIMIT, space=jax.ShapeDtypeStruct):
     return pl.pallas_call(
         functools.partial(split_kernel, first),
         in_specs=[HBM] + [ANY] * len(after),
         out_specs=ANY,
-        out_shape=jax.ShapeDtypeStruct((size,) + heads.shape[1:], heads.dtype),
+        out_shape=space((size,) + heads.shape[1:], heads.dtype),
         scratch_shapes=[
             pltpu.VMEM((size,) + heads.shape[1:], heads.dtype),
             pltpu.SemaphoreType.DMA((2,)),
@@ -356,7 +357,7 @@
     ends = jnp.stack([layer < gz_count - 1, layer > 0]).astype(jnp.float32)
 
     spans = [(2 * sum(CHUNKS[:c]), 2 * size) for c, size in enumerate(CHUNKS)]
-    parts = [split(heads, *spans[0])]
+    parts = [split(heads, *spans[0], space=pltpu.VMEM)]
     hot, *weights = prepare(
         misfit,
         row_owner,
@@ -370,15 +371,17 @@
         parts[0],
     )
     later = [split(heads, *span, after=[hot]) for span in spans[2:]]
-    parts += [split(heads, *spans[1], after=later), *later]
-    arrived = [(lax.ppermute(p, "gz", down), lax.ppermute(p, "gz", up)) for p in parts]
+    parts += [split(heads, *spans[1], after=[hot]), *later]
+    below = [lax.ppermute(p, "gz", up) for p in parts]
+    arrived = [(lax.ppermute(p, "gz", down), b) for p, b in zip(parts, below)]
     adjoint = None
-    order = [[hot], [], []]
+    order = [[hot, *parts[2:]], [], []]
     partials = []
     for c, (first, size) in enumerate(spans):
         resident = c < RESIDENT
-        matrix = load(x_inverse, parts[1] if c == 0 else lines) if resident else x_inverse
-        lines = x_sweep(heads, first, *arrived[c], leak, matrix, ends, order[c], resident)
+        matrix = load(x_inverse, parts[c + 1]) if resident else x_inverse
+        own, place = (parts[c], 0) if resident else (heads, first)
+        lines = x_sweep(own, place, *arrived[c], leak, matrix, ends, order[c], resident)
         swept = lines.reshape(gx_count, x_local, size * y_local)
         swept = lax.all_to_all(swept, "gx", split_axis=0, concat_axis=0, tiled=True)
         befores = partials if c == len(spans) - 1 else []

time: 159 us -> 157 us (0.987)
  local copies, waits for them, and re-layouts: 6.22 us -> 4.16 us
    pallas_call x1 -> x2, Pallas kernels: 3.54 us -> 7.17 us  [load(): pl.pallas_call(load_kernel, in_specs=[HBM, ANY], out_specs=VMEM, out_shap...]
    unnamed x26 -> x24, local copies, waits for them, and re-layouts: 5.99 us -> 3.93 us
  transfers between devices with their start and end apart: 12 -> 12, of which waited for: 9 -> 9; matrix products, arithmetic and copies ran while one was open for 0% -> 0% of each run, Pallas kernels for 36% -> 38%
where the time goes in v4:
time: 157 us
  Pallas kernels  66 us (42%)
  starting transfers between devices  36.8 us (23%)
  waiting for transfers between devices  30.2 us (19%)
  blocking collectives  17.1 us (11%)
  local copies, waits for them, and re-layouts  4.16 us (3%)
  between operations  1.62 us (1%)
    all_to_all x4, starting transfers between devices, body(): swept = lax.all_to_all(swept, 'gx', split_axis=0, concat_axis=0, tiled=True)  27.4 us
    pallas_call x4, Pallas kernels, x_sweep(): pl.pallas_call(functools.partial(x_kernel, first, len(after), resident),...  27.3 us
    pallas_call x4, Pallas kernels, y_sweep(): pl.pallas_call(functools.partial(y_kernel, first, len(befores)), in_specs...  23.5 us
    all_to_all x4, waiting for transfers between devices, body(): swept = lax.all_to_all(swept, 'gx', split_axis=0, concat_axis=0, tiled=True)  19.6 us
    all_to_all x1, blocking collectives, body(): lax.all_to_all(sent, ('gx', 'gz'), split_axis=0, concat_axis=0, tiled=True)  17.1 us
    pallas_call x2, Pallas kernels, load(): pl.pallas_call(load_kernel, in_specs=[HBM, ANY], out_specs=VMEM, out_shap...  7.17 us
    pallas_call x4, Pallas kernels, split(): pl.pallas_call(functools.partial(split_kernel, first), in_specs=[HBM] + [...  6.56 us
    ppermute x4, starting transfers between devices, body(): arrived = [(lax.ppermute(p, 'gz', down), b) for p, b in zip(parts, below)]  6.52 us
  transfers between devices with their start and end apart: 12, of which 9 were waited for; matrix products, arithmetic and copies ran while one was open for 0% of the time, Pallas kernels for 38%

profile of v4, /device:TPU:1, one launch (start us, length us, event | category | flops | bytes accessed | tf_op | source)
XLA Modules:
  0.0 156.7 jit_solution(7052200047228807182)
XLA Ops:
  0.7 1.3 split.4.after.own
  2.0 3.6 %collective-permute-start.2 = (bf16[4,1,64,2048]{3,2,1,0:T(8,128)(2,1)S(1)}, bf16[4,1,64,2048]{3,2,1,0:T(8,128)(2,1)}, u32[]{:S(2)}, u32[]{:S(2)}) collective-permute-start(bf16[4,1,64,2048]{3,2,1,0:T(8,128)(2,1)S(1)} %split.4.after.own), channel_id=1, source_target_pairs={{1,0},{2,1},{3,2},{0,3},{5,4},{6,5},{7,6},{4,7},{9,8},{10,9},{11,1... | collective-permute-start | bytes 3145736 | tf_op jit(solution)/shard_map/ppermute | solution.py:376
  5.6 0.0 collective-permute-start.3
  5.7 0.1 copy.14.cells
  6.5 1.5 prepare.1
  8.0 1.0 copy-done.4
  8.9 1.0 copy-done.5
  9.9 1.0 copy-done.6
  10.9 1.0 copy-done.7
  11.9 2.2 %split.6.after.own = bf16[4,1,64,2048]{3,2,1,0:T(8,128)(2,1)} custom-call(bf16[16,1,64,2048]{3,2,1,0:T(8,128)(2,1)} %own.3, bf16[256,1024]{1,0:T(8,128)(2,1)S(1)} %get-tuple-element.15.rest_0_.hot), custom_call_target="tpu_custom_call" | custom-call | bytes 2097152 | tf_op jit(solution)/shard_map/split/pallas_call | solution.py:50
  14.1 2.7 %collective-permute-start.4 = (bf16[4,1,64,2048]{3,2,1,0:T(8,128)(2,1)}, bf16[4,1,64,2048]{3,2,1,0:T(8,128)(2,1)}, u32[]{:S(2)}, u32[]{:S(2)}) collective-permute-start(bf16[4,1,64,2048]{3,2,1,0:T(8,128)(2,1)} %split.6.after.own), channel_id=1, source_target_pairs={{1,0},{2,1},{3,2},{0,3},{5,4},{6,5},{7,6},{4,7},{9,8},{10,9},{11,1... | collective-permute-start | bytes 3145736 | tf_op jit(solution)/shard_map/ppermute | solution.py:376
  16.8 0.0 collective-permute-start.5
  16.8 0.1 add_convert_fusion.ends
  16.9 1.3 split.7.rest_1_.after
  18.2 1.7 %split.5.rest_2_ = bf16[4,1,64,2048]{3,2,1,0:T(8,128)(2,1)S(1)} custom-call(bf16[16,1,64,2048]{3,2,1,0:T(8,128)(2,1)} %own.3, bf16[256,1024]{1,0:T(8,128)(2,1)S(1)} %get-tuple-element.15.rest_0_.hot), custom_call_target="tpu_custom_call" | custom-call | bytes 2097152 | tf_op jit(solution)/shard_map/split/pallas_call | solution.py:50
  20.0 0.0 copy-start.2
  20.0 0.0 copy-start.1
  20.0 3.8 %load.2.inverse = bf16[1,2048,2048]{2,1,0:T(8,128)(2,1)S(1)} custom-call(bf16[1,2048,2048]{2,1,0:T(8,128)(2,1)} %inverse.9, bf16[4,1,64,2048]{3,2,1,0:T(8,128)(2,1)} %split.6.after.own), custom_call_target="tpu_custom_call" | custom-call | bytes 16777216 | tf_op jit(solution)/shard_map/load/pallas_call | solution.py:70
  23.8 3.7 %collective-permute-done.2.above = bf16[4,1,64,2048]{3,2,1,0:T(8,128)(2,1)} collective-permute-done((bf16[4,1,64,2048]{3,2,1,0:T(8,128)(2,1)S(1)}, bf16[4,1,64,2048]{3,2,1,0:T(8,128)(2,1)}, u32[]{:S(2)}, u32[]{:S(2)}) %collective-permute-start.2) | collective-permute-done | bytes 1048608 | tf_op jit(solution)/shard_map/ppermute | solution.py:376
  27.5 3.2 %collective-permute-done.3.below = bf16[4,1,64,2048]{3,2,1,0:T(8,128)(2,1)} collective-permute-done((bf16[4,1,64,2048]{3,2,1,0:T(8,128)(2,1)S(1)}, bf16[4,1,64,2048]{3,2,1,0:T(8,128)(2,1)}, u32[]{:S(2)}, u32[]{:S(2)}) %collective-permute-start.3) | collective-permute-done | bytes 1048608 | tf_op jit(solution)/shard_map/ppermute | solution.py:375
  30.7 6.0 %x_sweep.4 = bf16[2048,256]{1,0:T(8,128)(2,1)} custom-call(f32[2]{0:T(128)S(1)} %add_convert_fusion.ends, bf16[4,1,64,2048]{3,2,1,0:T(8,128)(2,1)S(1)} %split.4.after.own, bf16[4,1,64,2048]{3,2,1,0:T(8,128)(2,1)} %collective-permute-done.2.above, bf16[4,1,64,2048]{3,2,1,0:T(8,128)(2,1)} %collective-permute-done.3.below, f32[1,64,2048]{2,1,0:T(8,128)S(1)} %copy-done.1, ...), custom_call_target="tpu_custom_call" | custom-call | flops 2147483648 | bytes 20971520 | tf_op jit(solution)/shard_map/x_sweep/pallas_call | solution.py:183
  36.7 11.3 %all-to-all-start = ((bf16[32,64,256]{2,1,0:T(8,128)(2,1)}), bf16[32,64,256]{2,1,0:T(8,128)(2,1)}, u32[]{:S(2)}, u32[]{:S(2)}) async-start(bf16[32,64,256]{2,1,0:T(8,128)(2,1)} %bitcast.17), calls=%async_computation | async-start | bytes 2097152 | tf_op jit(solution)/shard_map/all_to_all | solution.py:386
  48.0 0.1 collective-permute-start.6
  48.1 1.4 collective-permute-start.7
  49.5 3.4 %load.3.inverse = bf16[1,2048,2048]{2,1,0:T(8,128)(2,1)S(1)} custom-call(bf16[1,2048,2048]{2,1,0:T(8,128)(2,1)} %inverse.9, bf16[4,1,64,2048]{3,2,1,0:T(8,128)(2,1)} %copy-done), custom_call_target="tpu_custom_call" | custom-call | bytes 16777216 | tf_op jit(solution)/shard_map/load/pallas_call | solution.py:70
  52.9 0.0 copy-start.3
  53.0 0.2 collective-permute-done.5.below
  53.1 6.1 %x_sweep.6 = bf16[2048,256]{1,0:T(8,128)(2,1)} custom-call(f32[2]{0:T(128)S(1)} %add_convert_fusion.ends, bf16[4,1,64,2048]{3,2,1,0:T(8,128)(2,1)} %split.6.after.own, bf16[4,1,64,2048]{3,2,1,0:T(8,128)(2,1)} %collective-permute-done.4.above, bf16[4,1,64,2048]{3,2,1,0:T(8,128)(2,1)} %collective-permute-done.5.below, f32[1,64,2048]{2,1,0:T(8,128)S(1)} %copy-done.1, ...), custom_call_target="tpu_custom_call" | custom-call | flops 2147483648 | bytes 20971520 | tf_op jit(solution)/shard_map/x_sweep/pallas_call | solution.py:183
  59.2 6.0 %all-to-all-done.swept = bf16[32,64,256]{2,1,0:T(8,128)(2,1)} async-done(((bf16[32,64,256]{2,1,0:T(8,128)(2,1)}), bf16[32,64,256]{2,1,0:T(8,128)(2,1)}, u32[]{:S(2)}, u32[]{:S(2)}) %all-to-all-start) | async-done | bytes 1048608 | tf_op jit(solution)/shard_map/all_to_all | solution.py:386
  65.2 5.3 %all-to-all-start.2 = ((bf16[32,64,256]{2,1,0:T(8,128)(2,1)}), bf16[32,64,256]{2,1,0:T(8,128)(2,1)}, u32[]{:S(2)}, u32[]{:S(2)}) async-start(bf16[32,64,256]{2,1,0:T(8,128)(2,1)} %bitcast.16), calls=%async_computation.2 | async-start | bytes 2097152 | tf_op jit(solution)/shard_map/all_to_all | solution.py:386
  70.6 0.1 collective-permute-start
  70.7 1.5 collective-permute-start.1
  72.1 0.5 collective-permute-done.6.above
  72.6 3.0 %collective-permute-done.7.below = bf16[4,1,64,2048]{3,2,1,0:T(8,128)(2,1)} collective-permute-done((bf16[4,1,64,2048]{3,2,1,0:T(8,128)(2,1)S(1)}, bf16[4,1,64,2048]{3,2,1,0:T(8,128)(2,1)}, u32[]{:S(2)}, u32[]{:S(2)}) %collective-permute-start.7) | collective-permute-done | bytes 1048608 | tf_op jit(solution)/shard_map/ppermute | solution.py:375
  75.6 7.6 %x_sweep.7 = bf16[2048,256]{1,0:T(8,128)(2,1)} custom-call(f32[2]{0:T(128)S(1)} %add_convert_fusion.ends, bf16[16,1,64,2048]{3,2,1,0:T(8,128)(2,1)} %own.3, bf16[4,1,64,2048]{3,2,1,0:T(8,128)(2,1)} %collective-permute-done.6.above, bf16[4,1,64,2048]{3,2,1,0:T(8,128)(2,1)} %collective-permute-done.7.below, f32[1,64,2048]{2,1,0:T(8,128)S(1)} %copy-done.1, ...), custom_call_target="tpu_custom_call" | custom-call | flops 2147483648 | bytes 20971520 | tf_op jit(solution)/shard_map/x_sweep/pallas_call | solution.py:183
  83.2 4.6 %all-to-all-done.2.swept = bf16[32,64,256]{2,1,0:T(8,128)(2,1)} async-done(((bf16[32,64,256]{2,1,0:T(8,128)(2,1)}), bf16[32,64,256]{2,1,0:T(8,128)(2,1)}, u32[]{:S(2)}, u32[]{:S(2)}) %all-to-all-start.2) | async-done | bytes 1048608 | tf_op jit(solution)/shard_map/all_to_all | solution.py:386
  87.8 6.7 %all-to-all-start.3 = ((bf16[32,64,256]{2,1,0:T(8,128)(2,1)}), bf16[32,64,256]{2,1,0:T(8,128)(2,1)S(1)}, u32[]{:S(2)}, u32[]{:S(2)}) async-start(bf16[32,64,256]{2,1,0:T(8,128)(2,1)} %bitcast.18), calls=%async_computation.3 | async-start | bytes 2097152 | tf_op jit(solution)/shard_map/all_to_all | solution.py:386
  94.5 6.0 %y_sweep.4 = (bf16[16,1,64,2048]{3,2,1,0:T(8,128)(2,1)}, bf16[32,16,128]{2,1,0:T(8,128)(2,1)S(1)}) custom-call(bf16[32,64,256]{2,1,0:T(8,128)(2,1)} %all-to-all-done.swept, bf16[1,2048,2048]{2,1,0:T(8,128)(2,1)} %inverse.11, bf16[256,1024]{1,0:T(8,128)(2,1)S(1)} %get-tuple-element.15.rest_0_.hot, bf16[2,512,512]{2,1,0:T(8,128)(2,1)} %copy-done.4), custom_call_target="tpu_custom_call" | custom-call | flops 2147483648 | bytes 20971520 | tf_op jit(solution)/shard_map/y_sweep/pallas_call | solution.py:321
  100.6 7.6 %x_sweep.5 = bf16[2048,256]{1,0:T(8,128)(2,1)} custom-call(f32[2]{0:T(128)S(1)} %add_convert_fusion.ends, bf16[16,1,64,2048]{3,2,1,0:T(8,128)(2,1)} %own.3, bf16[4,1,64,2048]{3,2,1,0:T(8,128)(2,1)} %collective-permute-done.above, bf16[4,1,64,2048]{3,2,1,0:T(8,128)(2,1)} %collective-permute-done.1.below, f32[1,64,2048]{2,1,0:T(8,128)S(1)} %copy-done.1, ...), custom_call_target="tpu_custom_call" | custom-call | flops 2147483648 | bytes 20971520 | tf_op jit(solution)/shard_map/x_sweep/pallas_call | solution.py:183
  108.2 3.5 %all-to-all-done.3.swept = bf16[32,64,256]{2,1,0:T(8,128)(2,1)S(1)} async-done(((bf16[32,64,256]{2,1,0:T(8,128)(2,1)}), bf16[32,64,256]{2,1,0:T(8,128)(2,1)S(1)}, u32[]{:S(2)}, u32[]{:S(2)}) %all-to-all-start.3) | async-done | bytes 1048608 | tf_op jit(solution)/shard_map/all_to_all | solution.py:386
  111.7 4.0 %all-to-all-start.1 = ((bf16[32,64,256]{2,1,0:T(8,128)(2,1)}), bf16[32,64,256]{2,1,0:T(8,128)(2,1)S(1)}, u32[]{:S(2)}, u32[]{:S(2)}) async-start(bf16[32,64,256]{2,1,0:T(8,128)(2,1)} %bitcast.19), calls=%async_computation.1 | async-start | bytes 2097152 | tf_op jit(solution)/shard_map/all_to_all | solution.py:386
  115.7 6.0 %y_sweep.5 = (bf16[16,1,64,2048]{3,2,1,0:T(8,128)(2,1)}, bf16[32,16,128]{2,1,0:T(8,128)(2,1)S(1)}) custom-call(bf16[32,64,256]{2,1,0:T(8,128)(2,1)} %all-to-all-done.2.swept, bf16[1,2048,2048]{2,1,0:T(8,128)(2,1)} %inverse.11, bf16[256,1024]{1,0:T(8,128)(2,1)S(1)} %get-tuple-element.15.rest_0_.hot, ...), custom_call_target="tpu_custom_call", output_to_operand_aliasing={{0}: (4, {})} | custom-call | flops 2147483648 | bytes 20971520 | tf_op jit(solution)/shard_map/y_sweep/pallas_call | solution.py:321
  121.7 5.8 %y_sweep.6 = (bf16[16,1,64,2048]{3,2,1,0:T(8,128)(2,1)}, bf16[32,16,128]{2,1,0:T(8,128)(2,1)S(1)}) custom-call(bf16[32,64,256]{2,1,0:T(8,128)(2,1)S(1)} %all-to-all-done.3.swept, bf16[1,2048,2048]{2,1,0:T(8,128)(2,1)} %inverse.11, bf16[256,1024]{1,0:T(8,128)(2,1)S(1)} %get-tuple-element.15.rest_0_.hot, ...), custom_call_target="tpu_custom_call", output_to_operand_aliasing={{0}: (4, {})} | custom-call | flops 2147483648 | bytes 20971520 | tf_op jit(solution)/shard_map/y_sweep/pallas_call | solution.py:321
  127.5 5.5 %all-to-all-done.1.swept = bf16[32,64,256]{2,1,0:T(8,128)(2,1)S(1)} async-done(((bf16[32,64,256]{2,1,0:T(8,128)(2,1)}), bf16[32,64,256]{2,1,0:T(8,128)(2,1)S(1)}, u32[]{:S(2)}, u32[]{:S(2)}) %all-to-all-start.1) | async-done | bytes 1048608 | tf_op jit(solution)/shard_map/all_to_all | solution.py:386
  133.0 5.8 %y_sweep.7 = (bf16[16,1,64,2048]{3,2,1,0:T(8,128)(2,1)}, bf16[32,64,128]{2,1,0:T(8,128)(2,1)S(1)}) custom-call(bf16[32,64,256]{2,1,0:T(8,128)(2,1)S(1)} %all-to-all-done.1.swept, bf16[1,2048,2048]{2,1,0:T(8,128)(2,1)} %inverse.11, bf16[256,1024]{1,0:T(8,128)(2,1)S(1)} %get-tuple-element.15.rest_0_.hot, ...), custom_call_target="tpu_custom_call", output_to_operand_aliasing={{0}: (7, {})} | custom-call | flops 2147483648 | bytes 20971520 | tf_op jit(solution)/shard_map/y_sweep/pallas_call | solution.py:321
  138.8 0.1 copy.15
  138.9 17.1 %all_to_all.25 = bf16[128,16,128]{2,1,0:T(8,128)(2,1)S(1)} all-to-all(bf16[128,16,128]{2,1,0:T(8,128)(2,1)S(1)} %bitcast.20), channel_id=1, replica_groups=mesh['gx'=32,'gz'=4] {'gx','gz'}, dimensions={0} | all-to-all | bytes 1048576 | tf_op jit(solution)/shard_map/all_to_all | solution.py:404
  155.9 0.7 convert_reduce_fusion
  (22 shorter events, 0.1 us)
Async XLA Ops:
  0.6 5.0 %copy-start.10 = (s32[256]{0:T(256)S(1)}, s32[256]{0:T(256)}, u32[]{:S(2)}) copy-start(s32[256]{0:T(256)} %param.16) | copy-start | bytes 3076
  0.6 5.0 %copy-start.11 = (s32[256]{0:T(256)S(1)}, s32[256]{0:T(256)}, u32[]{:S(2)}) copy-start(s32[256]{0:T(256)} %param.17) | copy-start | bytes 3076
  0.7 5.2 %copy-start.9 = (f32[256,16]{0,1:T(8,128)S(1)}, f32[256,16]{0,1:T(8,128)}, u32[]{:S(2)}) copy-start(f32[256,16]{0,1:T(8,128)} %param.13) | copy-start | bytes 49156
  0.7 5.8 %copy-start.8 = (s32[256,1]{0,1:T(1,128)S(1)}, s32[256,1]{0,1:T(1,128)}, u32[]{:S(2)}) copy-start(s32[256,1]{0,1:T(1,128)} %param.14) | copy-start | bytes 3076
  2.0 25.5 %collective-permute-start.2 = (bf16[4,1,64,2048]{3,2,1,0:T(8,128)(2,1)S(1)}, bf16[4,1,64,2048]{3,2,1,0:T(8,128)(2,1)}, u32[]{:S(2)}, u32[]{:S(2)}) collective-permute-start(bf16[4,1,64,2048]{3,2,1,0:T(8,128)(2,1)S(1)} %split.4.after.own), channel_id=1, source_target_pairs={{1,0},{2,1},{3,2},{0,3},{5,4},{6,5},{7,6},{4,7},{9,8},{10,9},{11,1... | collective-permute-start | bytes 3145736 | tf_op jit(solution)/shard_map/ppermute | solution.py:376
  5.6 25.0 %collective-permute-start.3 = (bf16[4,1,64,2048]{3,2,1,0:T(8,128)(2,1)S(1)}, bf16[4,1,64,2048]{3,2,1,0:T(8,128)(2,1)}, u32[]{:S(2)}, u32[]{:S(2)}) collective-permute-start(bf16[4,1,64,2048]{3,2,1,0:T(8,128)(2,1)S(1)} %split.4.after.own), channel_id=1, source_target_pairs={{0,1},{1,2},{2,3},{3,0},{4,5},{5,6},{6,7},{7,4},{8,9},{9,10},{10,1... | collective-permute-start | bytes 3145736 | tf_op jit(solution)/shard_map/ppermute | solution.py:375
  8.0 1.0 copy-start.4
  8.9 1.0 copy-start.5
  9.9 1.0 copy-start.6
  10.9 1.0 copy-start.7
  14.1 38.8 %collective-permute-start.4 = (bf16[4,1,64,2048]{3,2,1,0:T(8,128)(2,1)}, bf16[4,1,64,2048]{3,2,1,0:T(8,128)(2,1)}, u32[]{:S(2)}, u32[]{:S(2)}) collective-permute-start(bf16[4,1,64,2048]{3,2,1,0:T(8,128)(2,1)} %split.6.after.own), channel_id=1, source_target_pairs={{1,0},{2,1},{3,2},{0,3},{5,4},{6,5},{7,6},{4,7},{9,8},{10,9},{11,1... | collective-permute-start | bytes 3145736 | tf_op jit(solution)/shard_map/ppermute | solution.py:376
  16.8 36.3 %collective-permute-start.5 = (bf16[4,1,64,2048]{3,2,1,0:T(8,128)(2,1)}, bf16[4,1,64,2048]{3,2,1,0:T(8,128)(2,1)}, u32[]{:S(2)}, u32[]{:S(2)}) collective-permute-start(bf16[4,1,64,2048]{3,2,1,0:T(8,128)(2,1)} %split.6.after.own), channel_id=1, source_target_pairs={{0,1},{1,2},{2,3},{3,0},{4,5},{5,6},{6,7},{7,4},{8,9},{9,10},{10,1... | collective-permute-start | bytes 3145736 | tf_op jit(solution)/shard_map/ppermute | solution.py:375
  18.2 29.8 %copy-start = (bf16[4,1,64,2048]{3,2,1,0:T(8,128)(2,1)}, bf16[4,1,64,2048]{3,2,1,0:T(8,128)(2,1)S(1)}, u32[]{:S(2)}) copy-start(bf16[4,1,64,2048]{3,2,1,0:T(8,128)(2,1)S(1)} %split.7.rest_1_.after) | copy-start | bytes 3145732
  20.0 10.7 %copy-start.2 = (bf16[4,1,64,2048]{3,2,1,0:T(8,128)(2,1)}, bf16[4,1,64,2048]{3,2,1,0:T(8,128)(2,1)S(1)}, u32[]{:S(2)}) copy-start(bf16[4,1,64,2048]{3,2,1,0:T(8,128)(2,1)S(1)} %split.5.rest_2_) | copy-start | bytes 3145732
  20.0 10.7 %copy-start.1 = (f32[1,64,2048]{2,1,0:T(8,128)S(1)}, f32[1,64,2048]{2,1,0:T(8,128)}, u32[]{:S(2)}) copy-start(f32[1,64,2048]{2,1,0:T(8,128)} %leak.7) | copy-start | bytes 1572868
  36.7 28.6 %all-to-all-start = ((bf16[32,64,256]{2,1,0:T(8,128)(2,1)}), bf16[32,64,256]{2,1,0:T(8,128)(2,1)}, u32[]{:S(2)}, u32[]{:S(2)}) async-start(bf16[32,64,256]{2,1,0:T(8,128)(2,1)} %bitcast.17), calls=%async_computation | async-start | bytes 2097152 | tf_op jit(solution)/shard_map/all_to_all | solution.py:386
  48.0 24.6 %collective-permute-start.6 = (bf16[4,1,64,2048]{3,2,1,0:T(8,128)(2,1)S(1)}, bf16[4,1,64,2048]{3,2,1,0:T(8,128)(2,1)}, u32[]{:S(2)}, u32[]{:S(2)}) collective-permute-start(bf16[4,1,64,2048]{3,2,1,0:T(8,128)(2,1)S(1)} %split.7.rest_1_.after), channel_id=1, source_target_pairs={{1,0},{2,1},{3,2},{0,3},{5,4},{6,5},{7,6},{4,7},{9,8},{10,9},{11,1... | collective-permute-start | bytes 3145736 | tf_op jit(solution)/shard_map/ppermute | solution.py:376
  48.1 27.5 %collective-permute-start.7 = (bf16[4,1,64,2048]{3,2,1,0:T(8,128)(2,1)S(1)}, bf16[4,1,64,2048]{3,2,1,0:T(8,128)(2,1)}, u32[]{:S(2)}, u32[]{:S(2)}) collective-permute-start(bf16[4,1,64,2048]{3,2,1,0:T(8,128)(2,1)S(1)} %split.7.rest_1_.after), channel_id=1, source_target_pairs={{0,1},{1,2},{2,3},{3,0},{4,5},{5,6},{6,7},{7,4},{8,9},{9,10},{10,1... | collective-permute-start | bytes 3145736 | tf_op jit(solution)/shard_map/ppermute | solution.py:375
  52.9 17.6 %copy-start.3 = (bf16[4,1,64,2048]{3,2,1,0:T(8,128)(2,1)S(1)}, bf16[4,1,64,2048]{3,2,1,0:T(8,128)(2,1)}, u32[]{:S(2)}) copy-start(bf16[4,1,64,2048]{3,2,1,0:T(8,128)(2,1)} %copy-done.2) | copy-start | bytes 3145732
  65.2 22.6 %all-to-all-start.2 = ((bf16[32,64,256]{2,1,0:T(8,128)(2,1)}), bf16[32,64,256]{2,1,0:T(8,128)(2,1)}, u32[]{:S(2)}, u32[]{:S(2)}) async-start(bf16[32,64,256]{2,1,0:T(8,128)(2,1)} %bitcast.16), calls=%async_computation.2 | async-start | bytes 2097152 | tf_op jit(solution)/shard_map/all_to_all | solution.py:386
  70.6 30.0 %collective-permute-start = (bf16[4,1,64,2048]{3,2,1,0:T(8,128)(2,1)S(1)}, bf16[4,1,64,2048]{3,2,1,0:T(8,128)(2,1)}, u32[]{:S(2)}, u32[]{:S(2)}) collective-permute-start(bf16[4,1,64,2048]{3,2,1,0:T(8,128)(2,1)S(1)} %copy-done.3), channel_id=1, source_target_pairs={{1,0},{2,1},{3,2},{0,3},{5,4},{6,5},{7,6},{4,7},{9,8},{10,9},{11,1... | collective-permute-start | bytes 3145736 | tf_op jit(solution)/shard_map/ppermute | solution.py:376
  70.7 29.9 %collective-permute-start.1 = (bf16[4,1,64,2048]{3,2,1,0:T(8,128)(2,1)S(1)}, bf16[4,1,64,2048]{3,2,1,0:T(8,128)(2,1)}, u32[]{:S(2)}, u32[]{:S(2)}) collective-permute-start(bf16[4,1,64,2048]{3,2,1,0:T(8,128)(2,1)S(1)} %copy-done.3), channel_id=1, source_target_pairs={{0,1},{1,2},{2,3},{3,0},{4,5},{5,6},{6,7},{7,4},{8,9},{9,10},{10,1... | collective-permute-start | bytes 3145736 | tf_op jit(solution)/shard_map/ppermute | solution.py:375
  87.8 23.9 %all-to-all-start.3 = ((bf16[32,64,256]{2,1,0:T(8,128)(2,1)}), bf16[32,64,256]{2,1,0:T(8,128)(2,1)S(1)}, u32[]{:S(2)}, u32[]{:S(2)}) async-start(bf16[32,64,256]{2,1,0:T(8,128)(2,1)} %bitcast.18), calls=%async_computation.3 | async-start | bytes 2097152 | tf_op jit(solution)/shard_map/all_to_all | solution.py:386
  111.7 21.3 %all-to-all-start.1 = ((bf16[32,64,256]{2,1,0:T(8,128)(2,1)}), bf16[32,64,256]{2,1,0:T(8,128)(2,1)S(1)}, u32[]{:S(2)}, u32[]{:S(2)}) async-start(bf16[32,64,256]{2,1,0:T(8,128)(2,1)} %bitcast.19), calls=%async_computation.1 | async-start | bytes 2097152 | tf_op jit(solution)/shard_map/all_to_all | solution.py:386

commit v5 on v4

--- a/solution.py
+++ b/solution.py
@@ -15,7 +15,7 @@
 Y_LIMIT = 52
 LOAD_LIMIT = 50
 RESIDENT_LIMIT = 24
-RESIDENT = 2
+RESIDENT = 3
 LAST_LIMIT = 51
 NT = (((1,), (1,)), ((), ()))
 MIB = 1 << 20

time: 157 us -> 157 us (level)
  waiting for transfers between devices: 30.2 us -> 26.8 us
  Pallas kernels: 66 us -> 68.2 us
    pallas_call x2 -> x3, Pallas kernels: 7.17 us -> 10.6 us  [load(): pl.pallas_call(load_kernel, in_specs=[HBM, ANY], out_specs=VMEM, out_shap...]
    ppermute x4, waiting for transfers between devices: 6.39 us -> 3.42 us  [body(): below = [lax.ppermute(p, 'gz', up) for p in parts]]
    ppermute x4, waiting for transfers between devices: 4.21 us -> 2.26 us  [body(): arrived = [(lax.ppermute(p, 'gz', down), b) for p, b in zip(parts, below)]]
    pallas_call x4, Pallas kernels: 27.3 us -> 25.7 us  [x_sweep(): pl.pallas_call(functools.partial(x_kernel, first, len(after), resident),...]
    unnamed x24 -> x20, local copies, waits for them, and re-layouts: 3.93 us -> 3.61 us
  transfers between devices with their start and end apart: 12 -> 12, of which waited for: 9 -> 8; matrix products, arithmetic and copies ran while one was open for 0% -> 1% of each run, Pallas kernels for 38% -> 39%
where the time goes in v5:
time: 157 us; the launch traced here: 156 us
  Pallas kernels  68.2 us (43%)
  starting transfers between devices  36.6 us (23%)
  waiting for transfers between devices  26.8 us (17%)
  blocking collectives  17.1 us (11%)
  local copies, waits for them, and re-layouts  4.56 us (3%)
  between operations  1.59 us (1%)
    all_to_all x4, starting transfers between devices, body(): swept = lax.all_to_all(swept, 'gx', split_axis=0, concat_axis=0, tiled=True)  27.2 us
    pallas_call x4, Pallas kernels, x_sweep(): pl.pallas_call(functools.partial(x_kernel, first, len(after), resident),...  25.7 us
    pallas_call x4, Pallas kernels, y_sweep(): pl.pallas_call(functools.partial(y_kernel, first, len(befores)), in_specs...  23.5 us
    all_to_all x4, waiting for transfers between devices, body(): swept = lax.all_to_all(swept, 'gx', split_axis=0, concat_axis=0, tiled=True)  21.1 us
    all_to_all x1, blocking collectives, body(): lax.all_to_all(sent, ('gx', 'gz'), split_axis=0, concat_axis=0, tiled=True)  17.1 us
    pallas_call x3, Pallas kernels, load(): pl.pallas_call(load_kernel, in_specs=[HBM, ANY], out_specs=VMEM, out_shap...  10.6 us
    pallas_call x4, Pallas kernels, split(): pl.pallas_call(functools.partial(split_kernel, first), in_specs=[HBM] + [...  6.91 us
    ppermute x4, starting transfers between devices, body(): arrived = [(lax.ppermute(p, 'gz', down), b) for p, b in zip(parts, below)]  6.53 us
  transfers between devices with their start and end apart: 12, of which 8 were waited for; matrix products, arithmetic and copies ran while one was open for 1% of the time, Pallas kernels for 39%

profile of v5, /device:TPU:1, one launch (start us, length us, event | category | flops | bytes accessed | tf_op | source)
XLA Modules:
  0.0 156.3 jit_solution(15854629171889329591)
XLA Ops:
  0.6 1.3 split.4.after.own
  2.0 3.6 %collective-permute-start.2 = (bf16[4,1,64,2048]{3,2,1,0:T(8,128)(2,1)S(1)}, bf16[4,1,64,2048]{3,2,1,0:T(8,128)(2,1)}, u32[]{:S(2)}, u32[]{:S(2)}) collective-permute-start(bf16[4,1,64,2048]{3,2,1,0:T(8,128)(2,1)S(1)} %split.4.after.own), channel_id=1, source_target_pairs={{1,0},{2,1},{3,2},{0,3},{5,4},{6,5},{7,6},{4,7},{9,8},{10,9},{11,1... | collective-permute-start | bytes 3145736 | tf_op jit(solution)/shard_map/ppermute | solution.py:376
  5.6 0.7 multiply_add_fusion
  6.3 0.1 copy.14.cells
  6.4 0.7 reshape.28.misfit
  7.8 0.0 copy-start.9
  7.8 0.7 copy-done.9
  8.5 1.5 prepare.1
  10.0 1.0 copy-done.5
  10.9 1.0 copy-done.7
  11.9 1.0 copy-done.8
  12.9 2.6 %split.6.after.own = bf16[4,1,64,2048]{3,2,1,0:T(8,128)(2,1)} custom-call(bf16[16,1,64,2048]{3,2,1,0:T(8,128)(2,1)} %own.1, bf16[256,1024]{1,0:T(8,128)(2,1)S(1)} %get-tuple-element.15.rest_0_.hot), custom_call_target="tpu_custom_call" | custom-call | bytes 2097152 | tf_op jit(solution)/shard_map/split/pallas_call | solution.py:50
  15.5 2.7 %collective-permute-start.4 = (bf16[4,1,64,2048]{3,2,1,0:T(8,128)(2,1)}, bf16[4,1,64,2048]{3,2,1,0:T(8,128)(2,1)}, u32[]{:S(2)}, u32[]{:S(2)}) collective-permute-start(bf16[4,1,64,2048]{3,2,1,0:T(8,128)(2,1)} %split.6.after.own), channel_id=1, source_target_pairs={{1,0},{2,1},{3,2},{0,3},{5,4},{6,5},{7,6},{4,7},{9,8},{10,9},{11,1... | collective-permute-start | bytes 3145736 | tf_op jit(solution)/shard_map/ppermute | solution.py:376
  18.2 0.1 add_convert_fusion.ends
  18.3 1.3 split.7.rest_1_.after.own
  19.6 1.7 %split.5.rest_2_.after = bf16[4,1,64,2048]{3,2,1,0:T(8,128)(2,1)S(1)} custom-call(bf16[16,1,64,2048]{3,2,1,0:T(8,128)(2,1)} %own.1, bf16[256,1024]{1,0:T(8,128)(2,1)S(1)} %get-tuple-element.15.rest_0_.hot), custom_call_target="tpu_custom_call" | custom-call | bytes 2097152 | tf_op jit(solution)/shard_map/split/pallas_call | solution.py:50
  21.3 0.0 copy-start.2
  21.4 0.0 copy-start.4
  21.4 3.8 %load.3.inverse = bf16[1,2048,2048]{2,1,0:T(8,128)(2,1)S(1)} custom-call(bf16[1,2048,2048]{2,1,0:T(8,128)(2,1)} %source.5, bf16[4,1,64,2048]{3,2,1,0:T(8,128)(2,1)} %split.6.after.own), custom_call_target="tpu_custom_call" | custom-call | bytes 16777216 | tf_op jit(solution)/shard_map/load/pallas_call | solution.py:70
  25.2 2.3 %collective-permute-done.2.above = bf16[4,1,64,2048]{3,2,1,0:T(8,128)(2,1)} collective-permute-done((bf16[4,1,64,2048]{3,2,1,0:T(8,128)(2,1)S(1)}, bf16[4,1,64,2048]{3,2,1,0:T(8,128)(2,1)}, u32[]{:S(2)}, u32[]{:S(2)}) %collective-permute-start.2) | collective-permute-done | bytes 1048608 | tf_op jit(solution)/shard_map/ppermute | solution.py:376
  27.4 3.2 %collective-permute-done.3.below = bf16[4,1,64,2048]{3,2,1,0:T(8,128)(2,1)} collective-permute-done((bf16[4,1,64,2048]{3,2,1,0:T(8,128)(2,1)S(1)}, bf16[4,1,64,2048]{3,2,1,0:T(8,128)(2,1)}, u32[]{:S(2)}, u32[]{:S(2)}) %collective-permute-start.3) | collective-permute-done | bytes 1048608 | tf_op jit(solution)/shard_map/ppermute | solution.py:375
  30.6 6.0 %x_sweep.4 = bf16[2048,256]{1,0:T(8,128)(2,1)} custom-call(f32[2]{0:T(128)S(1)} %add_convert_fusion.ends, bf16[4,1,64,2048]{3,2,1,0:T(8,128)(2,1)S(1)} %split.4.after.own, bf16[4,1,64,2048]{3,2,1,0:T(8,128)(2,1)} %collective-permute-done.2.above, bf16[4,1,64,2048]{3,2,1,0:T(8,128)(2,1)} %collective-permute-done.3.below, f32[1,64,2048]{2,1,0:T(8,128)S(1)} %copy-done.4, ...), custom_call_target="tpu_custom_call" | custom-call | flops 2147483648 | bytes 20971520 | tf_op jit(solution)/shard_map/x_sweep/pallas_call | solution.py:183
  36.6 11.3 %all-to-all-start = ((bf16[32,64,256]{2,1,0:T(8,128)(2,1)}), bf16[32,64,256]{2,1,0:T(8,128)(2,1)}, u32[]{:S(2)}, u32[]{:S(2)}) async-start(bf16[32,64,256]{2,1,0:T(8,128)(2,1)} %bitcast.18), calls=%async_computation | async-start | bytes 2097152 | tf_op jit(solution)/shard_map/all_to_all | solution.py:386
  48.0 0.1 collective-permute-start.6
  48.0 1.4 collective-permute-start.7
  49.5 3.4 %load.4.inverse = bf16[1,2048,2048]{2,1,0:T(8,128)(2,1)S(1)} custom-call(bf16[1,2048,2048]{2,1,0:T(8,128)(2,1)} %source.5, bf16[4,1,64,2048]{3,2,1,0:T(8,128)(2,1)} %copy-done), custom_call_target="tpu_custom_call" | custom-call | bytes 16777216 | tf_op jit(solution)/shard_map/load/pallas_call | solution.py:70
  52.9 0.2 collective-permute-done.5.below
  53.1 6.1 %x_sweep.6 = bf16[2048,256]{1,0:T(8,128)(2,1)} custom-call(f32[2]{0:T(128)S(1)} %add_convert_fusion.ends, bf16[4,1,64,2048]{3,2,1,0:T(8,128)(2,1)} %split.6.after.own, bf16[4,1,64,2048]{3,2,1,0:T(8,128)(2,1)} %collective-permute-done.4.above, bf16[4,1,64,2048]{3,2,1,0:T(8,128)(2,1)} %collective-permute-done.5.below, f32[1,64,2048]{2,1,0:T(8,128)S(1)} %copy-done.4, ...), custom_call_target="tpu_custom_call" | custom-call | flops 2147483648 | bytes 20971520 | tf_op jit(solution)/shard_map/x_sweep/pallas_call | solution.py:183
  59.2 6.0 %all-to-all-done.swept = bf16[32,64,256]{2,1,0:T(8,128)(2,1)} async-done(((bf16[32,64,256]{2,1,0:T(8,128)(2,1)}), bf16[32,64,256]{2,1,0:T(8,128)(2,1)}, u32[]{:S(2)}, u32[]{:S(2)}) %all-to-all-start) | async-done | bytes 1048608 | tf_op jit(solution)/shard_map/all_to_all | solution.py:386
  65.2 5.3 %all-to-all-start.2 = ((bf16[32,64,256]{2,1,0:T(8,128)(2,1)}), bf16[32,64,256]{2,1,0:T(8,128)(2,1)}, u32[]{:S(2)}, u32[]{:S(2)}) async-start(bf16[32,64,256]{2,1,0:T(8,128)(2,1)} %bitcast.16), calls=%async_computation.2 | async-start | bytes 2097152 | tf_op jit(solution)/shard_map/all_to_all | solution.py:386
  70.6 0.1 collective-permute-start
  70.6 1.5 collective-permute-start.1
  72.1 3.4 %load.5.inverse = bf16[1,2048,2048]{2,1,0:T(8,128)(2,1)S(1)} custom-call(bf16[1,2048,2048]{2,1,0:T(8,128)(2,1)} %source.5, bf16[4,1,64,2048]{3,2,1,0:T(8,128)(2,1)} %copy-done.2), custom_call_target="tpu_custom_call" | custom-call | bytes 16777216 | tf_op jit(solution)/shard_map/load/pallas_call | solution.py:70
  75.5 0.1 collective-permute-done.7.below
  75.6 6.0 %x_sweep.7 = bf16[2048,256]{1,0:T(8,128)(2,1)} custom-call(f32[2]{0:T(128)S(1)} %add_convert_fusion.ends, bf16[4,1,64,2048]{3,2,1,0:T(8,128)(2,1)S(1)} %copy-done.1, bf16[4,1,64,2048]{3,2,1,0:T(8,128)(2,1)} %collective-permute-done.6.above, bf16[4,1,64,2048]{3,2,1,0:T(8,128)(2,1)} %collective-permute-done.7.below, f32[1,64,2048]{2,1,0:T(8,128)S(1)} %copy-done.4, ...), custom_call_target="tpu_custom_call" | custom-call | flops 2147483648 | bytes 20971520 | tf_op jit(solution)/shard_map/x_sweep/pallas_call | solution.py:183
  81.6 6.2 %all-to-all-done.2.swept = bf16[32,64,256]{2,1,0:T(8,128)(2,1)} async-done(((bf16[32,64,256]{2,1,0:T(8,128)(2,1)}), bf16[32,64,256]{2,1,0:T(8,128)(2,1)}, u32[]{:S(2)}, u32[]{:S(2)}) %all-to-all-start.2) | async-done | bytes 1048608 | tf_op jit(solution)/shard_map/all_to_all | solution.py:386
  87.8 5.1 %all-to-all-start.3 = ((bf16[32,64,256]{2,1,0:T(8,128)(2,1)}), bf16[32,64,256]{2,1,0:T(8,128)(2,1)S(1)}, u32[]{:S(2)}, u32[]{:S(2)}) async-start(bf16[32,64,256]{2,1,0:T(8,128)(2,1)} %bitcast.17), calls=%async_computation.3 | async-start | bytes 2097152 | tf_op jit(solution)/shard_map/all_to_all | solution.py:386
  92.8 6.0 %y_sweep.4 = (bf16[16,1,64,2048]{3,2,1,0:T(8,128)(2,1)}, bf16[32,16,128]{2,1,0:T(8,128)(2,1)S(1)}) custom-call(bf16[32,64,256]{2,1,0:T(8,128)(2,1)} %all-to-all-done.swept, bf16[1,2048,2048]{2,1,0:T(8,128)(2,1)} %inverse.9, bf16[256,1024]{1,0:T(8,128)(2,1)S(1)} %get-tuple-element.15.rest_0_.hot, bf16[2,512,512]{2,1,0:T(8,128)(2,1)} %copy-done.5), custom_call_target="tpu_custom_call" | custom-call | flops 2147483648 | bytes 20971520 | tf_op jit(solution)/shard_map/y_sweep/pallas_call | solution.py:321
  98.9 7.6 %x_sweep.5 = bf16[2048,256]{1,0:T(8,128)(2,1)} custom-call(f32[2]{0:T(128)S(1)} %add_convert_fusion.ends, bf16[16,1,64,2048]{3,2,1,0:T(8,128)(2,1)} %own.1, bf16[4,1,64,2048]{3,2,1,0:T(8,128)(2,1)} %collective-permute-done.above, bf16[4,1,64,2048]{3,2,1,0:T(8,128)(2,1)} %collective-permute-done.1.below, f32[1,64,2048]{2,1,0:T(8,128)S(1)} %copy-done.4, ...), custom_call_target="tpu_custom_call" | custom-call | flops 2147483648 | bytes 20971520 | tf_op jit(solution)/shard_map/x_sweep/pallas_call | solution.py:183
  106.5 3.5 %all-to-all-done.3.swept = bf16[32,64,256]{2,1,0:T(8,128)(2,1)S(1)} async-done(((bf16[32,64,256]{2,1,0:T(8,128)(2,1)}), bf16[32,64,256]{2,1,0:T(8,128)(2,1)S(1)}, u32[]{:S(2)}, u32[]{:S(2)}) %all-to-all-start.3) | async-done | bytes 1048608 | tf_op jit(solution)/shard_map/all_to_all | solution.py:386
  110.0 5.4 %all-to-all-start.1 = ((bf16[32,64,256]{2,1,0:T(8,128)(2,1)}), bf16[32,64,256]{2,1,0:T(8,128)(2,1)S(1)}, u32[]{:S(2)}, u32[]{:S(2)}) async-start(bf16[32,64,256]{2,1,0:T(8,128)(2,1)} %bitcast.19), calls=%async_computation.1 | async-start | bytes 2097152 | tf_op jit(solution)/shard_map/all_to_all | solution.py:386
  115.5 6.0 %y_sweep.5 = (bf16[16,1,64,2048]{3,2,1,0:T(8,128)(2,1)}, bf16[32,16,128]{2,1,0:T(8,128)(2,1)S(1)}) custom-call(bf16[32,64,256]{2,1,0:T(8,128)(2,1)} %all-to-all-done.2.swept, bf16[1,2048,2048]{2,1,0:T(8,128)(2,1)} %inverse.9, bf16[256,1024]{1,0:T(8,128)(2,1)S(1)} %get-tuple-element.15.rest_0_.hot, ...), custom_call_target="tpu_custom_call", output_to_operand_aliasing={{0}: (4, {})} | custom-call | flops 2147483648 | bytes 20971520 | tf_op jit(solution)/shard_map/y_sweep/pallas_call | solution.py:321
  121.5 5.8 %y_sweep.6 = (bf16[16,1,64,2048]{3,2,1,0:T(8,128)(2,1)}, bf16[32,16,128]{2,1,0:T(8,128)(2,1)S(1)}) custom-call(bf16[32,64,256]{2,1,0:T(8,128)(2,1)S(1)} %all-to-all-done.3.swept, bf16[1,2048,2048]{2,1,0:T(8,128)(2,1)} %inverse.9, bf16[256,1024]{1,0:T(8,128)(2,1)S(1)} %get-tuple-element.15.rest_0_.hot, ...), custom_call_target="tpu_custom_call", output_to_operand_aliasing={{0}: (4, {})} | custom-call | flops 2147483648 | bytes 20971520 | tf_op jit(solution)/shard_map/y_sweep/pallas_call | solution.py:321
  127.2 5.4 %all-to-all-done.1.swept = bf16[32,64,256]{2,1,0:T(8,128)(2,1)S(1)} async-done(((bf16[32,64,256]{2,1,0:T(8,128)(2,1)}), bf16[32,64,256]{2,1,0:T(8,128)(2,1)S(1)}, u32[]{:S(2)}, u32[]{:S(2)}) %all-to-all-start.1) | async-done | bytes 1048608 | tf_op jit(solution)/shard_map/all_to_all | solution.py:386
  132.6 5.8 %y_sweep.7 = (bf16[16,1,64,2048]{3,2,1,0:T(8,128)(2,1)}, bf16[32,64,128]{2,1,0:T(8,128)(2,1)S(1)}) custom-call(bf16[32,64,256]{2,1,0:T(8,128)(2,1)S(1)} %all-to-all-done.1.swept, bf16[1,2048,2048]{2,1,0:T(8,128)(2,1)} %inverse.9, bf16[256,1024]{1,0:T(8,128)(2,1)S(1)} %get-tuple-element.15.rest_0_.hot, ...), custom_call_target="tpu_custom_call", output_to_operand_aliasing={{0}: (7, {})} | custom-call | flops 2147483648 | bytes 20971520 | tf_op jit(solution)/shard_map/y_sweep/pallas_call | solution.py:321
  138.4 0.1 copy.15
  138.5 17.1 %all_to_all.25 = bf16[128,16,128]{2,1,0:T(8,128)(2,1)S(1)} all-to-all(bf16[128,16,128]{2,1,0:T(8,128)(2,1)S(1)} %bitcast.20), channel_id=1, replica_groups=mesh['gx'=32,'gz'=4] {'gx','gz'}, dimensions={0} | all-to-all | bytes 1048576 | tf_op jit(solution)/shard_map/all_to_all | solution.py:404
  155.6 0.7 convert_reduce_fusion
  (19 shorter events, 0.0 us)
Async XLA Ops:
  2.0 25.5 %collective-permute-start.2 = (bf16[4,1,64,2048]{3,2,1,0:T(8,128)(2,1)S(1)}, bf16[4,1,64,2048]{3,2,1,0:T(8,128)(2,1)}, u32[]{:S(2)}, u32[]{:S(2)}) collective-permute-start(bf16[4,1,64,2048]{3,2,1,0:T(8,128)(2,1)S(1)} %split.4.after.own), channel_id=1, source_target_pairs={{1,0},{2,1},{3,2},{0,3},{5,4},{6,5},{7,6},{4,7},{9,8},{10,9},{11,1... | collective-permute-start | bytes 3145736 | tf_op jit(solution)/shard_map/ppermute | solution.py:376
  5.6 25.0 %collective-permute-start.3 = (bf16[4,1,64,2048]{3,2,1,0:T(8,128)(2,1)S(1)}, bf16[4,1,64,2048]{3,2,1,0:T(8,128)(2,1)}, u32[]{:S(2)}, u32[]{:S(2)}) collective-permute-start(bf16[4,1,64,2048]{3,2,1,0:T(8,128)(2,1)S(1)} %split.4.after.own), channel_id=1, source_target_pairs={{0,1},{1,2},{2,3},{3,0},{4,5},{5,6},{6,7},{7,4},{8,9},{9,10},{10,1... | collective-permute-start | bytes 3145736 | tf_op jit(solution)/shard_map/ppermute | solution.py:375
  7.8 0.7 copy-start.9
  10.0 1.0 copy-start.5
  10.9 1.0 copy-start.7
  11.9 1.0 copy-start.8
  12.9 5.3 %copy-start.6 = (bf16[2,512,512]{2,1,0:T(8,128)(2,1)}, bf16[2,512,512]{2,1,0:T(8,128)(2,1)S(1)}, u32[]{:S(2)}) copy-start(bf16[2,512,512]{2,1,0:T(8,128)(2,1)S(1)} %get-tuple-element.18.weights) | copy-start | bytes 3145732
  15.5 37.4 %collective-permute-start.4 = (bf16[4,1,64,2048]{3,2,1,0:T(8,128)(2,1)}, bf16[4,1,64,2048]{3,2,1,0:T(8,128)(2,1)}, u32[]{:S(2)}, u32[]{:S(2)}) collective-permute-start(bf16[4,1,64,2048]{3,2,1,0:T(8,128)(2,1)} %split.6.after.own), channel_id=1, source_target_pairs={{1,0},{2,1},{3,2},{0,3},{5,4},{6,5},{7,6},{4,7},{9,8},{10,9},{11,1... | collective-permute-start | bytes 3145736 | tf_op jit(solution)/shard_map/ppermute | solution.py:376
  18.2 34.9 %collective-permute-start.5 = (bf16[4,1,64,2048]{3,2,1,0:T(8,128)(2,1)}, bf16[4,1,64,2048]{3,2,1,0:T(8,128)(2,1)}, u32[]{:S(2)}, u32[]{:S(2)}) collective-permute-start(bf16[4,1,64,2048]{3,2,1,0:T(8,128)(2,1)} %split.6.after.own), channel_id=1, source_target_pairs={{0,1},{1,2},{2,3},{3,0},{4,5},{5,6},{6,7},{7,4},{8,9},{9,10},{10,1... | collective-permute-start | bytes 3145736 | tf_op jit(solution)/shard_map/ppermute | solution.py:375
  19.6 28.4 %copy-start = (bf16[4,1,64,2048]{3,2,1,0:T(8,128)(2,1)}, bf16[4,1,64,2048]{3,2,1,0:T(8,128)(2,1)S(1)}, u32[]{:S(2)}) copy-start(bf16[4,1,64,2048]{3,2,1,0:T(8,128)(2,1)S(1)} %split.7.rest_1_.after.own) | copy-start | bytes 3145732
  21.3 9.3 %copy-start.2 = (bf16[4,1,64,2048]{3,2,1,0:T(8,128)(2,1)}, bf16[4,1,64,2048]{3,2,1,0:T(8,128)(2,1)S(1)}, u32[]{:S(2)}) copy-start(bf16[4,1,64,2048]{3,2,1,0:T(8,128)(2,1)S(1)} %split.5.rest_2_.after) | copy-start | bytes 3145732
  21.4 9.3 %copy-start.4 = (f32[1,64,2048]{2,1,0:T(8,128)S(1)}, f32[1,64,2048]{2,1,0:T(8,128)}, u32[]{:S(2)}) copy-start(f32[1,64,2048]{2,1,0:T(8,128)} %leak.7) | copy-start | bytes 1572868
  36.6 28.6 %all-to-all-start = ((bf16[32,64,256]{2,1,0:T(8,128)(2,1)}), bf16[32,64,256]{2,1,0:T(8,128)(2,1)}, u32[]{:S(2)}, u32[]{:S(2)}) async-start(bf16[32,64,256]{2,1,0:T(8,128)(2,1)} %bitcast.18), calls=%async_computation | async-start | bytes 2097152 | tf_op jit(solution)/shard_map/all_to_all | solution.py:386
  48.0 27.5 %collective-permute-start.6 = (bf16[4,1,64,2048]{3,2,1,0:T(8,128)(2,1)S(1)}, bf16[4,1,64,2048]{3,2,1,0:T(8,128)(2,1)}, u32[]{:S(2)}, u32[]{:S(2)}) collective-permute-start(bf16[4,1,64,2048]{3,2,1,0:T(8,128)(2,1)S(1)} %split.7.rest_1_.after.own), channel_id=1, source_target_pairs={{1,0},{2,1},{3,2},{0,3},{5,4},{6,5},{7,6},{4,7},{9,8},{10,9},{11,1... | collective-permute-start | bytes 3145736 | tf_op jit(solution)/shard_map/ppermute | solution.py:376
  48.0 27.5 %collective-permute-start.7 = (bf16[4,1,64,2048]{3,2,1,0:T(8,128)(2,1)S(1)}, bf16[4,1,64,2048]{3,2,1,0:T(8,128)(2,1)}, u32[]{:S(2)}, u32[]{:S(2)}) collective-permute-start(bf16[4,1,64,2048]{3,2,1,0:T(8,128)(2,1)S(1)} %split.7.rest_1_.after.own), channel_id=1, source_target_pairs={{0,1},{1,2},{2,3},{3,0},{4,5},{5,6},{6,7},{7,4},{8,9},{9,10},{10,1... | collective-permute-start | bytes 3145736 | tf_op jit(solution)/shard_map/ppermute | solution.py:375
  52.9 17.6 %copy-start.3 = (bf16[4,1,64,2048]{3,2,1,0:T(8,128)(2,1)S(1)}, bf16[4,1,64,2048]{3,2,1,0:T(8,128)(2,1)}, u32[]{:S(2)}) copy-start(bf16[4,1,64,2048]{3,2,1,0:T(8,128)(2,1)} %copy-done.2) | copy-start | bytes 3145732
  65.2 22.6 %all-to-all-start.2 = ((bf16[32,64,256]{2,1,0:T(8,128)(2,1)}), bf16[32,64,256]{2,1,0:T(8,128)(2,1)}, u32[]{:S(2)}, u32[]{:S(2)}) async-start(bf16[32,64,256]{2,1,0:T(8,128)(2,1)} %bitcast.16), calls=%async_computation.2 | async-start | bytes 2097152 | tf_op jit(solution)/shard_map/all_to_all | solution.py:386
  70.5 5.0 %copy-start.1 = (bf16[4,1,64,2048]{3,2,1,0:T(8,128)(2,1)S(1)}, bf16[4,1,64,2048]{3,2,1,0:T(8,128)(2,1)}, u32[]{:S(2)}) copy-start(bf16[4,1,64,2048]{3,2,1,0:T(8,128)(2,1)} %copy-done) | copy-start | bytes 3145732
  70.6 28.3 %collective-permute-start = (bf16[4,1,64,2048]{3,2,1,0:T(8,128)(2,1)S(1)}, bf16[4,1,64,2048]{3,2,1,0:T(8,128)(2,1)}, u32[]{:S(2)}, u32[]{:S(2)}) collective-permute-start(bf16[4,1,64,2048]{3,2,1,0:T(8,128)(2,1)S(1)} %copy-done.3), channel_id=1, source_target_pairs={{1,0},{2,1},{3,2},{0,3},{5,4},{6,5},{7,6},{4,7},{9,8},{10,9},{11,1... | collective-permute-start | bytes 3145736 | tf_op jit(solution)/shard_map/ppermute | solution.py:376
  70.6 28.2 %collective-permute-start.1 = (bf16[4,1,64,2048]{3,2,1,0:T(8,128)(2,1)S(1)}, bf16[4,1,64,2048]{3,2,1,0:T(8,128)(2,1)}, u32[]{:S(2)}, u32[]{:S(2)}) collective-permute-start(bf16[4,1,64,2048]{3,2,1,0:T(8,128)(2,1)S(1)} %copy-done.3), channel_id=1, source_target_pairs={{0,1},{1,2},{2,3},{3,0},{4,5},{5,6},{6,7},{7,4},{8,9},{9,10},{10,1... | collective-permute-start | bytes 3145736 | tf_op jit(solution)/shard_map/ppermute | solution.py:375
  87.8 22.3 %all-to-all-start.3 = ((bf16[32,64,256]{2,1,0:T(8,128)(2,1)}), bf16[32,64,256]{2,1,0:T(8,128)(2,1)S(1)}, u32[]{:S(2)}, u32[]{:S(2)}) async-start(bf16[32,64,256]{2,1,0:T(8,128)(2,1)} %bitcast.17), calls=%async_computation.3 | async-start | bytes 2097152 | tf_op jit(solution)/shard_map/all_to_all | solution.py:386
  110.0 22.6 %all-to-all-start.1 = ((bf16[32,64,256]{2,1,0:T(8,128)(2,1)}), bf16[32,64,256]{2,1,0:T(8,128)(2,1)S(1)}, u32[]{:S(2)}, u32[]{:S(2)}) async-start(bf16[32,64,256]{2,1,0:T(8,128)(2,1)} %bitcast.19), calls=%async_computation.1 | async-start | bytes 2097152 | tf_op jit(solution)/shard_map/all_to_all | solution.py:386
